TPU v7x, 128 devices: a whole 4x4x4 slice. The times are simulated.
128 devices in a mesh: elem: 64 (over z, y, x), face: 2 (over core).
Axes of the slice: x: 4, y: 4, z: 4, core: 2. Of those that a mesh axis runs over, the one named last changes fastest.
Arguments:
- forcing: float32 [32768, 512], P(('elem', 'face')), may hold values from -15 to 15, as said below
- kappa: float32 [32768], P(('elem', 'face')), may hold values from 0.3 to 3
- elem_order: int32 [128, 256], P(('elem', 'face')), may hold values from 0 to 255, each once within a row
Outputs:
- solution: float32 [32768, 512], P(('elem', 'face'))
- residual: float32 [32768, 512], P(('elem', 'face'))
Inputs may be any that keep to these rules, and one draw needn't show every extreme that they name: `forcing`: element loads of order one, with a scale that varies by element and along z. `elem_order`: each row is a permutation of the 256 grid positions of the device's block.
All inputs are finite; a program needn't handle non-finite values.
Results may differ from a plain program's by a relative error of at most 0.0004.
Values sent between devices are 32-bit elements; how exact they have to be, the bound alone decides.
A program may use at most 192 MiB of HBM per device.

v0:
```python
import jax
import jax.numpy as jnp
import numpy as np
from jax import lax
from jax.sharding import PartitionSpec as P

EX = 8
EY = 32
EZ = 1
SWEEPS = 4
ITERS = 2


REACT = 0.02
OMEGA = 0.6


def padded_2(x, sides, width):
    for axis, dim in sides:
        size, length = (lax.axis_size(axis), x.shape[dim])
        up = [(i, (i + 1) % size) for i in range(size)]
        down = [(j, i) for i, j in up]
        last = lax.slice_in_dim(x, length - width, length, axis=dim)
        initial = lax.slice_in_dim(x, 0, width, axis=dim)
        before = lax.ppermute(last, axis, up)
        after = lax.ppermute(initial, axis, down)
        x = jnp.concatenate([before, x, after], axis=dim)
    return x


def from_behind(x, axis, by):
    size = lax.axis_size(axis)
    return lax.ppermute(x, axis, [(i, (i + by) % size) for i in range(size)])


def legendre_seven(points):
    before = np.ones(8)
    current = np.array(points)
    for degree in range(1, 7):
        following = ((2 * degree + 1) * points * current - degree * before) / (degree + 1)
        before = current
        current = following
    return current


def element_tables():
    points = np.array(
        [
            -1.0,
            -0.8717401485096066,
            -0.5917001814331423,
            -0.2092992179024789,
            0.2092992179024789,
            0.5917001814331423,
            0.8717401485096066,
            1.0,
        ]
    )
    weights = np.array(
        [
            1.0 / 28.0,
            0.2107042271435061,
            0.3411226924835044,
            0.4124587946587038,
            0.4124587946587038,
            0.3411226924835044,
            0.2107042271435061,
            1.0 / 28.0,
        ]
    )
    legendre = legendre_seven(points)
    derivative = np.zeros((8, 8))
    for left_node in range(8):
        for right_node in range(8):
            if left_node != right_node:
                derivative[left_node, right_node] = legendre[left_node] / (
                    legendre[right_node] * (points[left_node] - points[right_node])
                )
    derivative[0, 0] = -14.0
    derivative[7, 7] = 14.0
    stiffness = derivative.T @ (weights[:, None] * derivative)
    mass = np.eye(8) * weights[None, :]
    full_stiff = (
        np.kron(np.kron(mass, mass), stiffness)
        + np.kron(np.kron(mass, stiffness), mass)
        + np.kron(np.kron(stiffness, mass), mass)
    )
    mass_nodes = np.kron(np.kron(weights, weights), weights)
    interp = np.stack([(1.0 - points) / 2.0, (1.0 + points) / 2.0], 1)
    prolong = np.kron(np.kron(interp, interp), interp)
    coarse_stiff = prolong.T @ full_stiff @ prolong
    coarse_mass = prolong.T @ (mass_nodes[:, None] * prolong)
    ends = np.ones(8)
    ends[0] = 2.0
    ends[7] = 2.0
    inverse_mult = 1.0 / np.kron(np.kron(ends, ends), ends)
    return (
        stiffness,
        weights,
        full_stiff,
        mass_nodes,
        prolong,
        coarse_stiff,
        coarse_mass,
        inverse_mult,
    )


def pair_sum(grid, elem_axis, node_axis):
    upper = lax.index_in_dim(grid, 7, node_axis, keepdims=True)
    lower = lax.index_in_dim(grid, 0, node_axis, keepdims=True)
    shared = upper + jnp.roll(lower, -1, elem_axis)
    middle = lax.slice_in_dim(grid, 1, 7, axis=node_axis)
    return jnp.concatenate([jnp.roll(shared, 1, elem_axis), middle, shared], node_axis)


def direct_sum(field):
    grid = field.reshape(EZ, EY, EX, 8, 8, 8)
    grid = pair_sum(grid, 2, 5)
    grid = pair_sum(grid, 1, 4)
    upper = grid[:, :, :, 7]
    lower = grid[:, :, :, 0]
    rims = jnp.stack([lower[0], upper[-1]]).reshape(2, EY, EX * 64)
    padded = padded_2(rims, ((("elem", "face"), 0),), 1)
    below = padded[0].reshape(1, EY, EX, 8, 8)
    above = padded[3].reshape(1, EY, EX, 8, 8)
    shared = upper + jnp.concatenate([lower[1:], above], 0)
    first = jnp.concatenate([below, upper[:-1]], 0) + lower
    grid = jnp.concatenate([first[:, :, :, None], grid[:, :, :, 1:7], shared[:, :, :, None]], 3)
    return grid.reshape(-1, 512)


def vertex_corners(extended):
    planes = extended.shape[0] - 1
    parts = []
    for corner in range(8):
        along_z, along_y, along_x = (corner // 4, corner // 2 % 2, corner % 2)
        moved = jnp.roll(extended, (-along_y, -along_x), (1, 2))
        parts.append(moved[along_z : along_z + planes])
    return jnp.stack(parts, -1)


def with_next(vert):
    upper_plane = from_behind(vert[0], ("elem", "face"), -1)
    return jnp.concatenate([vert, upper_plane[None]], 0)


def raw_total(contrib):
    planes = contrib.shape[0]
    total = jnp.zeros((planes + 1,) + contrib.shape[1:3], jnp.float32)
    for corner in range(8):
        along_z, along_y, along_x = (corner // 4, corner // 2 % 2, corner % 2)
        moved = jnp.roll(contrib[..., corner], (along_y, along_x), (1, 2))
        total = total.at[along_z : along_z + planes].add(moved)
    return total


def local_assemble(contrib):
    planes = contrib.shape[0]
    total = raw_total(contrib)
    received = from_behind(total[planes], ("elem", "face"), 1)
    return total[:planes].at[0].add(received)


def per_device(forcing, kappa, elem_order):
    tabs = [jnp.asarray(table, jnp.float32) for table in element_tables()]
    stiffness, weights, full_stiff, mass_nodes = (tabs[0], tabs[1], tabs[2], tabs[3])
    prolong, coarse_stiff, coarse_mass, inverse_mult = (tabs[4], tabs[5], tabs[6], tabs[7])
    highest = lax.Precision.HIGHEST
    order = elem_order[0]
    count = order.shape[0]
    inverse = jnp.zeros((count,), jnp.int32).at[order].set(jnp.arange(count, dtype=jnp.int32))
    load = forcing[inverse]
    coeff = kappa[inverse]
    coeff_grid = coeff.reshape(EZ, EY, EX)
    corner_stiff = jnp.diag(coarse_stiff)
    corner_mass = jnp.diag(coarse_mass)
    diag_fine = direct_sum(
        coeff[:, None] * jnp.diag(full_stiff)[None, :] + REACT * mass_nodes[None, :]
    )
    coarse_diag = local_assemble(coeff_grid[..., None] * corner_stiff + REACT * corner_mass)

    def precondition(resid):
        restricted = jnp.dot(resid * inverse_mult[None, :], prolong, precision=highest).reshape(
            EZ, EY, EX, 8
        )
        target = local_assemble(restricted)
        vert = jnp.zeros_like(target)
        for sweep in range(SWEEPS):
            values = vertex_corners(with_next(vert)).reshape(-1, 8)
            contrib = coeff[:, None] * jnp.dot(
                values, coarse_stiff, precision=highest
            ) + REACT * jnp.dot(values, coarse_mass, precision=highest)
            vert = (
                vert
                + OMEGA * (target - local_assemble(contrib.reshape(EZ, EY, EX, 8))) / coarse_diag
            )
        extended = with_next(vert)
        values = vertex_corners(extended).reshape(-1, 8)
        return resid / diag_fine + jnp.dot(values, prolong.T, precision=highest)

    def inner(left, right):
        return jnp.sum(left * right * inverse_mult[None, :])

    def progress(resid, precond):
        return lax.psum(inner(resid, precond), ("elem", "face"))

    resid = direct_sum(load)
    solution = jnp.zeros_like(resid)
    precond = precondition(resid)
    direction = precond
    gamma = progress(resid, precond)
    for step in range(ITERS):
        cube = direction.reshape(-1, 8, 8, 8)
        term_x = jnp.einsum("xa,ecba->ecbx", stiffness, cube, precision=highest) * (
            weights[:, None, None] * weights[None, :, None]
        )
        term_y = jnp.einsum("yb,ecba->ecya", stiffness, cube, precision=highest) * (
            weights[:, None, None] * weights[None, None, :]
        )
        term_z = jnp.einsum("zc,ecba->ezba", stiffness, cube, precision=highest) * (
            weights[None, :, None] * weights[None, None, :]
        )
        local = (
            coeff[:, None] * (term_x + term_y + term_z).reshape(-1, 512)
            + REACT * mass_nodes[None, :] * direction
        )
        image = direct_sum(local)
        alpha = gamma / lax.psum(inner(direction, image), ("elem", "face"))
        solution = solution + alpha * direction
        resid = resid - alpha * image
        if step + 1 < ITERS:
            precond = precondition(resid)
            gamma_new = progress(resid, precond)
            direction = precond + gamma_new / gamma * direction
            gamma = gamma_new
    return (solution[order], resid[order])


def solution(mesh):
    in_specs = (P(("elem", "face"), None), P(("elem", "face")), P(("elem", "face"), None))
    out_specs = (P(("elem", "face"), None), P(("elem", "face"), None))
    return jax.shard_map(
        per_device, mesh=mesh, in_specs=in_specs, out_specs=out_specs, check_vma=False
    )
```

profile of v0, /device:TPU:1, one launch (start us, length us, event | category | flops | bytes accessed | tf_op | source)
XLA Modules:
  0.0 625.3 jit_solution(14336288162986129668)
XLA Ops:
  11.5 9.1 %slice.4087 = f32[1,32,8,8,8,1]{5,4,3,2,1,0:T(8,128)} slice(f32[1,32,8,8,8,8]{5,4,3,2,1,0:T(8,128)} %reshape.3978), slice={[0:1], [0:32], [0:8], [0:8], [0:8], [7:8]} | slice | bytes 131072 | tf_op jit(solution)/shard_map/slice | solution.py:110
  53.9 7.1 %collective-permute-start.1 = (f32[1,32,512]{1,2,0:T(8,128)S(1)}, f32[1,32,512]{1,2,0:T(8,128)S(1)}, u32[]{:S(2)}, u32[]{:S(2)}) collective-permute-start(f32[1,32,512]{1,2,0:T(8,128)S(1)} %bitcast.616), channel_id=1, source_target_pairs={{1,0},{2,1},{3,2},{4,3},{5,4},{6,5},{7,6},{8,7},{9,8},{10,9},{11,1... | collective-permute-start | bytes 196616 | tf_op jit(solution)/shard_map/ppermute | solution.py:26
  95.4 7.8 %collective-permute-start.8 = (f32[32,8]{0,1:T(8,128)S(1)}, f32[32,8]{0,1:T(8,128)S(1)}, u32[]{:S(2)}, u32[]{:S(2)}) collective-permute-start(f32[32,8]{0,1:T(8,128)S(1)} %get-tuple-element.1163), channel_id=1, source_target_pairs={{0,127},{1,0},{2,1},{3,2},{4,3},{5,4},{6,5},{7,6},{8,7},{9,8},{10,... | collective-permute-start | bytes 3080 | tf_op jit(solution)/shard_map/ppermute | solution.py:33
  115.3 7.8 %collective-permute-start.10 = (f32[32,8]{0,1:T(8,128)S(1)}, f32[32,8]{0,1:T(8,128)S(1)}, u32[]{:S(2)}, u32[]{:S(2)}) collective-permute-start(f32[32,8]{0,1:T(8,128)S(1)} %fusion.143), channel_id=1, source_target_pairs={{0,127},{1,0},{2,1},{3,2},{4,3},{5,4},{6,5},{7,6},{8,7},{9,8},{10,... | collective-permute-start | bytes 3080 | tf_op jit(solution)/shard_map/ppermute | solution.py:33
  130.9 7.5 %collective-permute-start.12 = (f32[32,8]{0,1:T(8,128)S(1)}, f32[32,8]{0,1:T(8,128)S(1)}, u32[]{:S(2)}, u32[]{:S(2)}) collective-permute-start(f32[32,8]{0,1:T(8,128)S(1)} %fusion.152), channel_id=1, source_target_pairs={{0,127},{1,0},{2,1},{3,2},{4,3},{5,4},{6,5},{7,6},{8,7},{9,8},{10,... | collective-permute-start | bytes 3080 | tf_op jit(solution)/shard_map/ppermute | solution.py:33
  143.8 7.4 %collective-permute-start.14 = (f32[32,8]{0,1:T(8,128)S(1)}, f32[32,8]{0,1:T(8,128)S(1)}, u32[]{:S(2)}, u32[]{:S(2)}) collective-permute-start(f32[32,8]{0,1:T(8,128)S(1)} %fusion.161), channel_id=1, source_target_pairs={{0,127},{1,0},{2,1},{3,2},{4,3},{5,4},{6,5},{7,6},{8,7},{9,8},{10,... | collective-permute-start | bytes 3080 | tf_op jit(solution)/shard_map/ppermute | solution.py:33
  154.2 7.3 %copy.829 = f32[1,32,8,8,8,8]{5,4,3,2,1,0:T(8,128)} copy(f32[1,32,8,8,8,8]{1,5,4,3,2,0:T(8,128)S(1)} %pad_maximum_fusion) | data formatting | bytes 1048576 | tf_op jit(solution)/shard_map/concatenate | solution.py:129
  168.3 8.2 %copy.831 = f32[1,32,8,8,8,8]{5,4,3,2,1,0:T(8,128)} copy(f32[1,32,8,8,8,8]{1,5,4,2,3,0:T(8,128)} %pad_maximum_fusion.1) | data formatting | bytes 1048576 | tf_op jit(solution)/shard_map/concatenate | solution.py:129
  176.6 7.6 %reshape.3980 = f32[256,512]{1,0:T(8,128)} reshape(f32[1,32,8,8,8,8]{5,4,3,2,1,0:T(8,128)} %copy.831) | data formatting | bytes 1048576 | tf_op jit(solution)/shard_map/reshape | solution.py:130
  197.8 7.5 %reshape.3988 = f32[1,32,8,8,8,8]{5,4,3,2,1,0:T(8,128)} reshape(f32[256,512]{1,0:T(8,128)} %multiply_add_fusion.18) | data formatting | bytes 1048576 | tf_op jit(solution)/shard_map/reshape | solution.py:118
  205.4 9.1 %slice.4267 = f32[1,32,8,8,8,1]{5,4,3,2,1,0:T(8,128)} slice(f32[1,32,8,8,8,8]{5,4,3,2,1,0:T(8,128)} %reshape.3988), slice={[0:1], [0:32], [0:8], [0:8], [0:8], [7:8]} | slice | bytes 131072 | tf_op jit(solution)/shard_map/slice | solution.py:110
  224.9 7.0 %copy.1053 = f32[1,32,8,8,8,1]{1,4,5,3,2,0:T(8,128)} copy(f32[1,32,8,8,8,1]{5,4,3,2,1,0:T(8,128)} %slice.4267) | data formatting | bytes 131072
  241.5 7.4 %copy.938 = f32[1,32,8,8,8,6]{1,5,4,3,2,0:T(8,128)} copy(f32[1,32,8,8,8,6]{5,4,3,2,1,0:T(8,128)} %slice.4272) | data formatting | bytes 786432 | tf_op jit(solution)/shard_map/slice | solution.py:113
  260.7 8.3 %copy.944 = f32[1,32,8,8,8,8]{5,4,3,2,1,0:T(8,128)} copy(f32[1,32,8,8,8,8]{1,5,4,3,2,0:T(8,128)} %pad_maximum_fusion.2) | data formatting | bytes 1048576 | tf_op jit(solution)/shard_map/concatenate | solution.py:129
  269.1 7.6 %reshape.3989 = f32[256,512]{1,0:T(8,128)} reshape(f32[1,32,8,8,8,8]{5,4,3,2,1,0:T(8,128)} %copy.944) | data formatting | bytes 1048576 | tf_op jit(solution)/shard_map/reshape | solution.py:130
  278.5 71.7 %all-reduce.1 = (f32[]{:T(128)}, f32[]{:T(128)}) all-reduce(f32[]{:T(128)} %get-tuple-element.1155, f32[]{:T(128)} %get-tuple-element.1154), channel_id=1, replica_groups=mesh['elem'=64,'face'=2] {'elem','face'}, use_global_device_ids=true, to_apply=%region_2.3 | all-reduce | flops 2 | bytes 16 | tf_op jit(solution)/shard_map/psum | solution.py:206
  357.1 7.8 %collective-permute-start.18 = (f32[32,8]{0,1:T(8,128)S(1)}, f32[32,8]{0,1:T(8,128)S(1)}, u32[]{:S(2)}, u32[]{:S(2)}) collective-permute-start(f32[32,8]{0,1:T(8,128)S(1)} %get-tuple-element.1161), channel_id=1, source_target_pairs={{0,127},{1,0},{2,1},{3,2},{4,3},{5,4},{6,5},{7,6},{8,7},{9,8},{10,... | collective-permute-start | bytes 3080 | tf_op jit(solution)/shard_map/ppermute | solution.py:33
  369.9 7.8 %collective-permute-start.20 = (f32[32,8]{0,1:T(8,128)S(1)}, f32[32,8]{0,1:T(8,128)S(1)}, u32[]{:S(2)}, u32[]{:S(2)}) collective-permute-start(f32[32,8]{0,1:T(8,128)S(1)} %fusion.170), channel_id=1, source_target_pairs={{0,127},{1,0},{2,1},{3,2},{4,3},{5,4},{6,5},{7,6},{8,7},{9,8},{10,... | collective-permute-start | bytes 3080 | tf_op jit(solution)/shard_map/ppermute | solution.py:33
  382.6 7.8 %collective-permute-start.22 = (f32[32,8]{0,1:T(8,128)S(1)}, f32[32,8]{0,1:T(8,128)S(1)}, u32[]{:S(2)}, u32[]{:S(2)}) collective-permute-start(f32[32,8]{0,1:T(8,128)S(1)} %fusion.179), channel_id=1, source_target_pairs={{0,127},{1,0},{2,1},{3,2},{4,3},{5,4},{6,5},{7,6},{8,7},{9,8},{10,... | collective-permute-start | bytes 3080 | tf_op jit(solution)/shard_map/ppermute | solution.py:33
  395.3 7.8 %collective-permute-start.24 = (f32[32,8]{0,1:T(8,128)S(1)}, f32[32,8]{0,1:T(8,128)S(1)}, u32[]{:S(2)}, u32[]{:S(2)}) collective-permute-start(f32[32,8]{0,1:T(8,128)S(1)} %fusion.188), channel_id=1, source_target_pairs={{0,127},{1,0},{2,1},{3,2},{4,3},{5,4},{6,5},{7,6},{8,7},{9,8},{10,... | collective-permute-start | bytes 3080 | tf_op jit(solution)/shard_map/ppermute | solution.py:33
  407.4 66.9 %psum.30 = f32[]{:T(128)} all-reduce(f32[]{:T(128)} %get-tuple-element.1158), channel_id=1, replica_groups=mesh['elem'=64,'face'=2] {'elem','face'}, use_global_device_ids=true, to_apply=%region_6.7 | all-reduce | flops 1 | bytes 8 | tf_op jit(solution)/shard_map/psum | solution.py:206
  484.9 9.1 %slice.4398 = f32[1,32,8,8,8,1]{5,4,3,2,1,0:T(8,128)} slice(f32[1,32,8,8,8,8]{5,4,3,2,1,0:T(8,128)} %reshape.3995), slice={[0:1], [0:32], [0:8], [0:8], [0:8], [7:8]} | slice | bytes 131072 | tf_op jit(solution)/shard_map/slice | solution.py:110
  532.1 7.3 %copy.1035 = f32[1,32,8,8,8,8]{5,4,3,2,1,0:T(8,128)} copy(f32[1,32,8,8,8,8]{1,5,4,3,2,0:T(8,128)S(1)} %pad_maximum_fusion.3) | data formatting | bytes 1048576 | tf_op jit(solution)/shard_map/concatenate | solution.py:129
  547.1 72.7 %psum.31 = f32[]{:T(128)} all-reduce(f32[]{:T(128)} %multiply_reduce_fusion), channel_id=1, replica_groups=mesh['elem'=64,'face'=2] {'elem','face'}, use_global_device_ids=true, to_apply=%region_8.9 | all-reduce | flops 1 | bytes 8 | tf_op jit(solution)/shard_map/psum | solution.py:229
  (794 shorter events, 242.2 us)
Async XLA Ops:
  0.7 75.1 %collective-permute-start.5 = (f32[32,8]{0,1:T(8,128)S(1)}, f32[32,8]{0,1:T(8,128)S(1)}, u32[]{:S(2)}, u32[]{:S(2)}) collective-permute-start(f32[32,8]{0,1:T(8,128)S(1)} %broadcast.1378), channel_id=1, source_target_pairs={{0,127},{1,0},{2,1},{3,2},{4,3},{5,4},{6,5},{7,6},{8,7},{9,8},{10,... | collective-permute-start | bytes 3080 | tf_op jit(solution)/shard_map/ppermute | solution.py:33
  52.7 29.5 %collective-permute-start = (f32[1,32,512]{1,2,0:T(8,128)}, f32[1,32,512]{1,2,0:T(8,128)S(1)}, u32[]{:S(2)}, u32[]{:S(2)}) collective-permute-start(f32[1,32,512]{1,2,0:T(8,128)} %bitcast.4), channel_id=1, source_target_pairs={{0,1},{1,2},{2,3},{3,4},{4,5},{5,6},{6,7},{7,8},{8,9},{9,10},{10,1... | collective-permute-start | bytes 196616 | tf_op jit(solution)/shard_map/ppermute | solution.py:25
  53.9 28.3 %collective-permute-start.1 = (f32[1,32,512]{1,2,0:T(8,128)S(1)}, f32[1,32,512]{1,2,0:T(8,128)S(1)}, u32[]{:S(2)}, u32[]{:S(2)}) collective-permute-start(f32[1,32,512]{1,2,0:T(8,128)S(1)} %bitcast.616), channel_id=1, source_target_pairs={{1,0},{2,1},{3,2},{4,3},{5,4},{6,5},{7,6},{8,7},{9,8},{10,9},{11,1... | collective-permute-start | bytes 196616 | tf_op jit(solution)/shard_map/ppermute | solution.py:26
  65.5 20.7 %collective-permute-start.7 = (f32[32,8]{0,1:T(8,128)}, f32[32,8]{0,1:T(8,128)}, u32[]{:S(2)}, u32[]{:S(2)}) collective-permute-start(f32[32,8]{0,1:T(8,128)} %fusion.122), channel_id=1, source_target_pairs={{0,1},{1,2},{2,3},{3,4},{4,5},{5,6},{6,7},{7,8},{8,9},{9,10},{10,1... | collective-permute-start | bytes 3080 | tf_op jit(solution)/shard_map/ppermute | solution.py:33
  79.9 8.2 %collective-permute-start.6 = (f32[32,8]{0,1:T(8,128)}, f32[32,8]{0,1:T(8,128)}, u32[]{:S(2)}, u32[]{:S(2)}) collective-permute-start(f32[32,8]{0,1:T(8,128)} %fusion.136), channel_id=1, source_target_pairs={{0,1},{1,2},{2,3},{3,4},{4,5},{5,6},{6,7},{7,8},{8,9},{9,10},{10,1... | collective-permute-start | bytes 3080 | tf_op jit(solution)/shard_map/ppermute | solution.py:33
  86.2 7.8 %collective-permute-start.4 = (f32[32,8]{0,1:T(8,128)S(1)}, f32[32,8]{0,1:T(8,128)S(1)}, u32[]{:S(2)}, u32[]{:S(2)}) collective-permute-start(f32[32,8]{0,1:T(8,128)S(1)} %fusion.131), channel_id=1, source_target_pairs={{0,1},{1,2},{2,3},{3,4},{4,5},{5,6},{6,7},{7,8},{8,9},{9,10},{10,1... | collective-permute-start | bytes 3080 | tf_op jit(solution)/shard_map/ppermute | solution.py:33
  95.4 9.6 %collective-permute-start.8 = (f32[32,8]{0,1:T(8,128)S(1)}, f32[32,8]{0,1:T(8,128)S(1)}, u32[]{:S(2)}, u32[]{:S(2)}) collective-permute-start(f32[32,8]{0,1:T(8,128)S(1)} %get-tuple-element.1163), channel_id=1, source_target_pairs={{0,127},{1,0},{2,1},{3,2},{4,3},{5,4},{6,5},{7,6},{8,7},{9,8},{10,... | collective-permute-start | bytes 3080 | tf_op jit(solution)/shard_map/ppermute | solution.py:33
  104.3 34.1 %collective-permute-start.2 = (f32[1,32,512]{1,2,0:T(8,128)S(1)}, f32[1,32,512]{1,2,0:T(8,128)S(1)}, u32[]{:S(2)}, u32[]{:S(2)}) collective-permute-start(f32[1,32,512]{1,2,0:T(8,128)S(1)} %bitcast.614), channel_id=1, source_target_pairs={{0,1},{1,2},{2,3},{3,4},{4,5},{5,6},{6,7},{7,8},{8,9},{9,10},{10,1... | collective-permute-start | bytes 196616 | tf_op jit(solution)/shard_map/ppermute | solution.py:25
  104.4 34.1 %collective-permute-start.3 = (f32[1,32,512]{1,2,0:T(8,128)S(1)}, f32[1,32,512]{1,2,0:T(8,128)S(1)}, u32[]{:S(2)}, u32[]{:S(2)}) collective-permute-start(f32[1,32,512]{1,2,0:T(8,128)S(1)} %bitcast.612), channel_id=1, source_target_pairs={{1,0},{2,1},{3,2},{4,3},{5,4},{6,5},{7,6},{8,7},{9,8},{10,9},{11,1... | collective-permute-start | bytes 196616 | tf_op jit(solution)/shard_map/ppermute | solution.py:26
  107.9 7.3 %collective-permute-start.9 = (f32[32,8]{0,1:T(8,128)S(1)}, f32[32,8]{0,1:T(8,128)S(1)}, u32[]{:S(2)}, u32[]{:S(2)}) collective-permute-start(f32[32,8]{0,1:T(8,128)S(1)} %fusion.145), channel_id=1, source_target_pairs={{0,1},{1,2},{2,3},{3,4},{4,5},{5,6},{6,7},{7,8},{8,9},{9,10},{10,1... | collective-permute-start | bytes 3080 | tf_op jit(solution)/shard_map/ppermute | solution.py:33
  115.3 11.5 %collective-permute-start.10 = (f32[32,8]{0,1:T(8,128)S(1)}, f32[32,8]{0,1:T(8,128)S(1)}, u32[]{:S(2)}, u32[]{:S(2)}) collective-permute-start(f32[32,8]{0,1:T(8,128)S(1)} %fusion.143), channel_id=1, source_target_pairs={{0,127},{1,0},{2,1},{3,2},{4,3},{5,4},{6,5},{7,6},{8,7},{9,8},{10,... | collective-permute-start | bytes 3080 | tf_op jit(solution)/shard_map/ppermute | solution.py:33
  130.9 8.8 %collective-permute-start.12 = (f32[32,8]{0,1:T(8,128)S(1)}, f32[32,8]{0,1:T(8,128)S(1)}, u32[]{:S(2)}, u32[]{:S(2)}) collective-permute-start(f32[32,8]{0,1:T(8,128)S(1)} %fusion.152), channel_id=1, source_target_pairs={{0,127},{1,0},{2,1},{3,2},{4,3},{5,4},{6,5},{7,6},{8,7},{9,8},{10,... | collective-permute-start | bytes 3080 | tf_op jit(solution)/shard_map/ppermute | solution.py:33
  143.8 40.6 %collective-permute-start.14 = (f32[32,8]{0,1:T(8,128)S(1)}, f32[32,8]{0,1:T(8,128)S(1)}, u32[]{:S(2)}, u32[]{:S(2)}) collective-permute-start(f32[32,8]{0,1:T(8,128)S(1)} %fusion.161), channel_id=1, source_target_pairs={{0,127},{1,0},{2,1},{3,2},{4,3},{5,4},{6,5},{7,6},{8,7},{9,8},{10,... | collective-permute-start | bytes 3080 | tf_op jit(solution)/shard_map/ppermute | solution.py:33
  252.5 3.4 collective-permute-start.15
  252.6 5.9 collective-permute-start.16
  355.2 1.8 collective-permute-start.17
  357.1 8.6 %collective-permute-start.18 = (f32[32,8]{0,1:T(8,128)S(1)}, f32[32,8]{0,1:T(8,128)S(1)}, u32[]{:S(2)}, u32[]{:S(2)}) collective-permute-start(f32[32,8]{0,1:T(8,128)S(1)} %get-tuple-element.1161), channel_id=1, source_target_pairs={{0,127},{1,0},{2,1},{3,2},{4,3},{5,4},{6,5},{7,6},{8,7},{9,8},{10,... | collective-permute-start | bytes 3080 | tf_op jit(solution)/shard_map/ppermute | solution.py:33
  368.7 1.2 collective-permute-start.19
  369.9 8.6 %collective-permute-start.20 = (f32[32,8]{0,1:T(8,128)S(1)}, f32[32,8]{0,1:T(8,128)S(1)}, u32[]{:S(2)}, u32[]{:S(2)}) collective-permute-start(f32[32,8]{0,1:T(8,128)S(1)} %fusion.170), channel_id=1, source_target_pairs={{0,127},{1,0},{2,1},{3,2},{4,3},{5,4},{6,5},{7,6},{8,7},{9,8},{10,... | collective-permute-start | bytes 3080 | tf_op jit(solution)/shard_map/ppermute | solution.py:33
  381.4 1.2 collective-permute-start.21
  382.6 8.6 %collective-permute-start.22 = (f32[32,8]{0,1:T(8,128)S(1)}, f32[32,8]{0,1:T(8,128)S(1)}, u32[]{:S(2)}, u32[]{:S(2)}) collective-permute-start(f32[32,8]{0,1:T(8,128)S(1)} %fusion.179), channel_id=1, source_target_pairs={{0,127},{1,0},{2,1},{3,2},{4,3},{5,4},{6,5},{7,6},{8,7},{9,8},{10,... | collective-permute-start | bytes 3080 | tf_op jit(solution)/shard_map/ppermute | solution.py:33
  395.3 8.6 %collective-permute-start.24 = (f32[32,8]{0,1:T(8,128)S(1)}, f32[32,8]{0,1:T(8,128)S(1)}, u32[]{:S(2)}, u32[]{:S(2)}) collective-permute-start(f32[32,8]{0,1:T(8,128)S(1)} %fusion.188), channel_id=1, source_target_pairs={{0,127},{1,0},{2,1},{3,2},{4,3},{5,4},{6,5},{7,6},{8,7},{9,8},{10,... | collective-permute-start | bytes 3080 | tf_op jit(solution)/shard_map/ppermute | solution.py:33
  525.8 3.4 collective-permute-start.25
  525.9 5.9 collective-permute-start.26
  (71 other events, 831.2 us)
where the time goes:
time: 636 us; the launch traced here: 625 us
  local copies, waits for them, and re-layouts  252 us (40%)
  blocking collectives  211 us (33%)
  starting transfers between devices  75.4 us (12%)
  other arithmetic  37.6 us (6%)
  waiting for transfers between devices  30.9 us (5%)
  matrix products  10.5 us (2%)
  between operations  7.45 us (1%)
    psum x2, blocking collectives, progress(): return lax.psum(inner(resid, precond), ('elem', 'face'))  139 us
    psum x1, blocking collectives, per_device(): alpha = gamma / lax.psum(inner(direction, image), ('elem', 'face'))  72.7 us
    ppermute x19, starting transfers between devices, from_behind(): return lax.ppermute(x, axis, [(i, (i + by) % size) for i in range(size)])  64.7 us
    unnamed x228, local copies, waits for them, and re-layouts  50.6 us
    slice x7, local copies, waits for them, and re-layouts, pair_sum(): middle = lax.slice_in_dim(grid, 1, 7, axis=node_axis)  37.8 us
    concatenate x4, local copies, waits for them, and re-layouts, direct_sum(): jnp.concatenate([first[:, :, :, None], grid[:, :, :, 1:7], shared[:, :, :...  31.1 us
    reshape x4, local copies, waits for them, and re-layouts, direct_sum(): return grid.reshape(-1, 512)  29 us
    slice x3, local copies, waits for them, and re-layouts, pair_sum(): upper = lax.index_in_dim(grid, 7, node_axis, keepdims=True)  27.3 us
  transfers between devices with their start and end apart: 27, of which 17 were waited for; matrix products, arithmetic and copies ran while one was open for 19% of the time, Pallas kernels for 0%

commit v1 on v0

v1 whole, which is shorter than its diff:
```python
import functools

import jax
import jax.numpy as jnp
import numpy as np
from jax import lax
from jax.experimental import pallas as pl
from jax.experimental.pallas import tpu as pltpu
from jax.sharding import PartitionSpec as P

EX = 8
EY = 32
ROWS = EX * EY
NODES = 512
REACT = 0.02
OMEGA = 0.6
REACH = 4
GROUP = 8
MESH = pl.DeviceIdType.MESH
F32 = jnp.float32
BF16 = jnp.bfloat16


def legendre_seven(points):
    before = np.ones(8)
    current = np.array(points)
    for degree in range(1, 7):
        following = ((2 * degree + 1) * points * current - degree * before) / (degree + 1)
        before = current
        current = following
    return current


def element_tables():
    points = np.array(
        [
            -1.0,
            -0.8717401485096066,
            -0.5917001814331423,
            -0.2092992179024789,
            0.2092992179024789,
            0.5917001814331423,
            0.8717401485096066,
            1.0,
        ]
    )
    weights = np.array(
        [
            1.0 / 28.0,
            0.2107042271435061,
            0.3411226924835044,
            0.4124587946587038,
            0.4124587946587038,
            0.3411226924835044,
            0.2107042271435061,
            1.0 / 28.0,
        ]
    )
    legendre = legendre_seven(points)
    derivative = np.zeros((8, 8))
    for left_node in range(8):
        for right_node in range(8):
            if left_node != right_node:
                derivative[left_node, right_node] = legendre[left_node] / (
                    legendre[right_node] * (points[left_node] - points[right_node])
                )
    derivative[0, 0] = -14.0
    derivative[7, 7] = 14.0
    stiffness = derivative.T @ (weights[:, None] * derivative)
    mass = np.eye(8) * weights[None, :]
    full_stiff = (
        np.kron(np.kron(mass, mass), stiffness)
        + np.kron(np.kron(mass, stiffness), mass)
        + np.kron(np.kron(stiffness, mass), mass)
    )
    mass_nodes = np.kron(np.kron(weights, weights), weights)
    interp = np.stack([(1.0 - points) / 2.0, (1.0 + points) / 2.0], 1)
    prolong = np.kron(np.kron(interp, interp), interp)
    return full_stiff, mass_nodes, prolong


def diagonal_tables(full_stiff, mass_nodes):
    diag = np.diag(full_stiff).reshape(8, 8, 8)
    mass = mass_nodes.reshape(8, 8, 8)
    share = np.zeros((32, 8, 8, 8))
    fixed = np.zeros((8, 8, 8))

    def ends(offset):
        if offset == 0:
            return list(range(8)), list(range(8))
        return ([7], [0]) if offset == 1 else ([0], [7])

    for index in range(27):
        offsets = (index // 9 - 1, index // 3 % 3 - 1, index % 3 - 1)
        mine = np.ix_(*[ends(offset)[0] for offset in offsets])
        theirs = np.ix_(*[ends(offset)[1] for offset in offsets])
        share[index][mine] += diag[theirs]
        fixed[mine] += REACT * mass[theirs]
    return share.reshape(32, NODES), fixed.reshape(1, NODES)


def split(value, pieces):
    parts = []
    for _ in range(pieces):
        part = value.astype(BF16)
        parts.append(part)
        value = value - part.astype(F32)
    return parts


def dot(left, right, dims=((1,), (0,))):
    return lax.dot_general(
        left, right, (dims, ((), ())), precision=lax.Precision.HIGHEST, preferred_element_type=F32
    )


def dot16(left, right, dims=((1,), (0,))):
    return lax.dot_general(left, right, (dims, ((), ())), preferred_element_type=F32)


def lanes(shape):
    return lax.broadcasted_iota(jnp.int32, shape, len(shape) - 1)


def roll_x(plane, by):
    size = plane.shape[1]
    along = lanes(plane.shape) % EX
    inside = pltpu.roll(plane, by % size, 1)
    around = pltpu.roll(plane, (by - EX * by) % size, 1)
    return jnp.where(along == (0 if by == 1 else EX - 1), around, inside)


def roll_y(plane, by):
    return pltpu.roll(plane, (by * EX) % plane.shape[1], 1)


def down(plane):
    return pltpu.roll(plane, plane.shape[0] - 1, 0)


def up(plane):
    return pltpu.roll(plane, 1, 0)


def shared_xy(tile):
    cube = tile.reshape(EY, EX, 128)
    lane = lanes(cube.shape)
    nx, ny = lane % 8, lane // 8 % 8
    after = pltpu.roll(pltpu.roll(cube, EX - 1, 1), 7, 2)
    before = pltpu.roll(pltpu.roll(cube, 1, 1), 128 - 7, 2)
    cube = cube + jnp.where(nx == 7, after, jnp.where(nx == 0, before, 0.0))
    after = pltpu.roll(jnp.concatenate([cube[1:], cube[:1]], 0), 56, 2)
    before = pltpu.roll(jnp.concatenate([cube[-1:], cube[:-1]], 0), 128 - 56, 2)
    cube = cube + jnp.where(ny == 7, after, jnp.where(ny == 0, before, 0.0))
    return cube.reshape(ROWS, 128)


def kernel(
    size,
    forcing_ref,
    kappa_ref,
    order_ref,
    stiff_ref,
    mass_ref,
    prolong_ref,
    share_ref,
    fixed_ref,
    solution_ref,
    residual_ref,
    r0_ref,
    z0_ref,
    q_ref,
    y_ref,
    w_ref,
    inverse_ref,
    coeff_ref,
    edge_out,
    edge_in,
    kap,
    rest,
    sum_a,
    sum_b,
    kap_send,
    kap_recv,
    rest_send,
    rest_recv,
    edge_send,
    edge_recv,
    a_send,
    a_recv,
    b_send,
    b_recv,
):
    me = lax.axis_index("elem") * 2 + lax.axis_index("face")
    groups = size // GROUP
    mine, place = lax.div(me, GROUP), lax.rem(me, GROUP)

    def ident(device):
        return lax.div(device, 2), lax.rem(device, 2)

    def ring(by):
        return ident(lax.rem(me + by + size, size))

    def group_mate(by):
        return ident(mine * GROUP + lax.rem(place + by, GROUP))

    def far_mate(by):
        return ident(lax.rem(mine + by, groups) * GROUP + place)

    near = [by for by in range(-REACH, REACH + 1) if by != 0]
    barrier = pltpu.get_barrier_semaphore()
    partners = [ring(by) for by in near]
    partners += [group_mate(by) for by in range(1, GROUP)]
    partners += [far_mate(by) for by in range(1, groups)]
    for partner in partners:
        pl.semaphore_signal(barrier, inc=1, device_id=partner, device_id_type=MESH)

    def remote(source, target, send, recv, device):
        return pltpu.make_async_remote_copy(
            src_ref=source,
            dst_ref=target,
            send_sem=send,
            recv_sem=recv,
            device_id=device,
            device_id_type=MESH,
        )

    def halo(buffer, send, recv):
        return [
            remote(
                buffer.at[REACH],
                buffer.at[REACH - by],
                send.at[REACH - by],
                recv.at[REACH - by],
                ring(by),
            )
            for by in near
        ]

    row = lax.broadcasted_iota(jnp.int32, (ROWS, ROWS), 0)
    pick = jnp.where(row == order_ref[...], 1.0, 0.0)
    pick16 = pick.astype(BF16)
    back16 = pick.T.astype(BF16)

    def permuted(matrix, value):
        return sum(dot16(matrix, part) for part in split(value, 3))

    kappa_rows = jnp.broadcast_to(kappa_ref[...], (16, ROWS))
    kappa_grid = sum(
        dot16(part, pick16, ((1,), (1,))) for part in split(kappa_rows, 3)
    )
    pl.semaphore_wait(barrier, len(partners))
    kap[REACH] = kappa_grid[0:1]
    kap_copies = halo(kap, kap_send, kap_recv)
    for copy in kap_copies:
        copy.start()

    load = permuted(pick16, forcing_ref[...])
    prolong = prolong_ref[...]

    def restrict(value, turn):
        each = dot(prolong, value, ((1,), (1,)))
        corner = lax.broadcasted_iota(jnp.int32, each.shape, 0)
        each = jnp.where(corner % 2 == 1, roll_x(each, 1), each)
        each = jnp.where(corner // 2 % 2 == 1, roll_y(each, 1), each)
        low = jnp.sum(each[0:4], axis=0, keepdims=True)
        high = jnp.sum(each[4:8], axis=0, keepdims=True)
        rest[turn, REACH] = jnp.concatenate([low, high], 0)
        copies = halo(rest.at[turn], rest_send.at[turn], rest_recv.at[turn])
        for copy in copies:
            copy.start()
        return copies

    half = lanes((ROWS // 2, 128)) < 64

    def faces(value, turn, target_ref):
        first = shared_xy(value[:, 0:128])
        last = shared_xy(value[:, 384:512])
        top, bottom = last[0:128], last[128:256]
        edge_out[turn, 0] = jnp.where(half, pltpu.roll(top, 64, 1), bottom)
        top, bottom = first[0:128], first[128:256]
        edge_out[turn, 1] = jnp.where(half, top, pltpu.roll(bottom, 64, 1))
        copies = [
            remote(
                edge_out.at[turn, way],
                edge_in.at[turn, way],
                edge_send.at[turn, way],
                edge_recv.at[turn, way],
                ring(by),
            )
            for way, by in ((0, 1), (1, -1))
        ]
        for copy in copies:
            copy.start()
        target_ref[:, 0:128] = first
        target_ref[:, 384:512] = last
        target_ref[:, 128:256] = shared_xy(value[:, 128:256])
        target_ref[:, 256:384] = shared_xy(value[:, 256:384])
        return copies

    def join(copies, turn, target_ref):
        for copy in copies:
            copy.wait_recv()
        below = edge_in[turn, 0]
        above = edge_in[turn, 1]
        zero = jnp.zeros_like(below)
        target_ref[0:128, 0:128] += jnp.where(half, below, zero)
        target_ref[128:256, 0:128] += jnp.where(half, pltpu.roll(below, 64, 1), zero)
        target_ref[0:128, 384:512] += jnp.where(half, zero, pltpu.roll(above, 64, 1))
        target_ref[128:256, 384:512] += jnp.where(half, zero, above)

    rest_copies = [restrict(load, 0)]
    edge_copies = [faces(load, 0, r0_ref)]

    for copy in kap_copies:
        copy.wait_recv()
    layers = [kap[m] for m in range(2 * REACH + 1)]
    under = jnp.concatenate(layers[:-1], 0)
    over = jnp.concatenate(layers[1:], 0)

    def four(layer):
        moved = [layer, roll_x(layer, 1)]
        return moved + [roll_y(moved[0], 1), roll_y(moved[1], 1)]

    under4, over4 = four(under), four(over)
    both4 = [a + b for a, b in zip(under4, over4)]
    diag = (2.0 / 3.0) * (both4[0] + both4[1] + both4[2] + both4[3]) + REACT * 64.0 / 27.0
    damp = -OMEGA / diag
    damp_down, damp_up = up(damp), down(damp)

    def stencil(layer4, planes):
        found = {}
        for dy in (-1, 0, 1):
            for dx in (-1, 0, 1):
                rows = (0, 1) if dy == 0 else ((0,) if dy == 1 else (1,))
                cols = (0, 1) if dx == 0 else ((0,) if dx == 1 else (1,))
                differ = abs(dy) + abs(dx) + (1 - planes)
                count = len(rows) * len(cols) * (1 + planes)
                weight = REACT * count * 2.0 ** (3 - differ) / 27.0
                if differ >= 2:
                    total = sum(layer4[2 * a + b] for a in rows for b in cols)
                    found[dy, dx] = (-1.0 / 6.0) * total + weight
                elif differ == 1:
                    found[dy, dx] = weight
        return found

    level = {key: damp * value for key, value in stencil(both4, 1).items()}
    from_above = {key: damp_down * value for key, value in stencil(under4, 0).items()}
    from_below = {key: damp_up * value for key, value in stencil(over4, 0).items()}

    def coarse(copies, turn):
        for copy in copies:
            copy.wait_recv()
        arrived = [rest[turn, m] for m in range(2 * REACH + 1)]
        target = jnp.concatenate([block[0:1] for block in arrived[1:]], 0) + jnp.concatenate(
            [block[1:2] for block in arrived[:-1]], 0
        )
        start = -damp * target
        vert = start
        for _ in range(3):
            along = {0: vert, 1: roll_x(vert, -1), -1: roll_x(vert, 1)}
            spread = {}
            for dx, value in along.items():
                spread[0, dx] = value
                spread[1, dx] = roll_y(value, -1)
                spread[-1, dx] = roll_y(value, 1)
            total = start + (1.0 - OMEGA) * vert
            total += sum(level[key] * spread[key] for key in level)
            total += down(sum(from_above[key] * spread[key] for key in from_above))
            total += up(sum(from_below[key] * spread[key] for key in from_below))
            vert = total
        one = roll_x(vert, -1)
        corners = [vert, one, roll_y(vert, -1), roll_y(one, -1)]
        return jnp.concatenate(
            [c[REACH - 1 : REACH] for c in corners] + [c[REACH : REACH + 1] for c in corners], 0
        )

    column = jnp.broadcast_to(kap[REACH], (8, ROWS)).T
    coeff_ref[...] = jnp.broadcast_to(column[:, 0:1], (ROWS, 128))
    around = []
    for m in (REACH - 1, REACH, REACH + 1):
        layer = jnp.broadcast_to(kap[m], (8, ROWS))
        side = {0: layer, 1: roll_x(layer, -1), -1: roll_x(layer, 1)}
        for dy in (-1, 0, 1):
            for dx in (-1, 0, 1):
                around.append(side[dx] if dy == 0 else roll_y(side[dx], -dy))
    around = jnp.concatenate([a[0:1] for a in around] + [jnp.zeros((5, ROWS), F32)], 0)
    inverse_ref[...] = 1.0 / (dot(around.T, share_ref[...]) + fixed_ref[...])

    def apply(value_ref, target_ref):
        product = dot(value_ref[...], stiff_ref[...])
        for tile in range(4):
            at = pl.ds(128 * tile, 128)
            target_ref[:, at] = (
                coeff_ref[...] * product[:, 128 * tile : 128 * tile + 128]
                + mass_ref[:, at] * value_ref[:, at]
            )
        return target_ref[...]

    def total(value):
        return jnp.sum(value.reshape(ROWS // 8, 8, 4, 128), axis=(0, 2))

    join(edge_copies[0], 0, r0_ref)
    corners = coarse(rest_copies[0], 0)
    z0_ref[...] = r0_ref[...] * inverse_ref[...] + dot(corners.T, prolong)
    z0 = z0_ref[...]
    partial = [total(load * z0)]
    image = apply(z0_ref, q_ref)
    rest_copies.append(restrict(image, 1))
    edge_copies.append(faces(image, 1, q_ref))
    partial.append(total(image * z0))
    join(edge_copies[1], 1, q_ref)
    corners = coarse(rest_copies[1], 1)
    y_ref[...] = q_ref[...] * inverse_ref[...] + dot(corners.T, prolong)
    y = y_ref[...]
    partial.append(total(image * y))
    image = apply(y_ref, w_ref)
    partial.append(total(image * y))

    which = lax.broadcasted_iota(jnp.int32, (8, 128), 0)
    sums = jnp.zeros((8, 128), F32)
    for index, value in enumerate(partial):
        sums = jnp.where(which == index, jnp.sum(value, axis=0, keepdims=True), sums)
    sum_a[0] = sums
    a_copies = [
        remote(sum_a.at[0], sum_a.at[by], a_send.at[by], a_recv.at[by], group_mate(by))
        for by in range(1, GROUP)
    ]
    for copy in a_copies:
        copy.start()
    edge_copies.append(faces(image, 2, w_ref))
    for copy in a_copies:
        copy.wait_recv()
    sum_b[0] = sum(sum_a[by] for by in range(GROUP))
    b_copies = [
        remote(sum_b.at[0], sum_b.at[by], b_send.at[by], b_recv.at[by], far_mate(by))
        for by in range(1, groups)
    ]
    for copy in b_copies:
        copy.start()
    join(edge_copies[2], 2, w_ref)
    for copy in b_copies:
        copy.wait_recv()
    sums = jnp.sum(sum(sum_b[by] for by in range(groups)), axis=1, keepdims=True)
    rz, zq, qy, yw = (sums[index : index + 1] for index in range(4))
    first = rz / zq
    gamma = first * first * qy - rz
    grown = 1.0 + gamma / rz
    second = gamma / (grown * grown * zq - 2.0 * first * grown * qy + first * first * yw)
    straight, bent = first + second * grown, first * second
    solution_ref[...] = permuted(back16, straight * z0_ref[...] - bent * y_ref[...])
    residual_ref[...] = permuted(
        back16, r0_ref[...] - straight * q_ref[...] + bent * w_ref[...]
    )

    for copies in [kap_copies, a_copies, b_copies] + rest_copies + edge_copies:
        for copy in copies:
            copy.wait_send()


def per_device(size, forcing, kappa, elem_order):
    full_stiff, mass_nodes, prolong = element_tables()
    share, fixed = diagonal_tables(full_stiff, mass_nodes)
    tables = [full_stiff, REACT * mass_nodes[None, :], prolong.T, share, fixed]
    groups = size // GROUP
    field = jax.ShapeDtypeStruct((ROWS, NODES), F32)
    count = 2 * REACH + 1
    dma = pltpu.SemaphoreType.DMA
    return pl.pallas_call(
        functools.partial(kernel, size),
        out_shape=(field, field),
        in_specs=[pl.BlockSpec(memory_space=pltpu.VMEM)] * 8,
        out_specs=(pl.BlockSpec(memory_space=pltpu.VMEM),) * 2,
        scratch_shapes=[pltpu.VMEM((ROWS, NODES), F32)] * 6
        + [
            pltpu.VMEM((ROWS, 128), F32),
            pltpu.VMEM((3, 2, 128, 128), F32),
            pltpu.VMEM((3, 2, 128, 128), F32),
            pltpu.VMEM((count, 1, ROWS), F32),
            pltpu.VMEM((2, count, 2, ROWS), F32),
            pltpu.VMEM((GROUP, 8, 128), F32),
            pltpu.VMEM((groups, 8, 128), F32),
            dma((count,)),
            dma((count,)),
            dma((2, count)),
            dma((2, count)),
            dma((3, 2)),
            dma((3, 2)),
            dma((GROUP,)),
            dma((GROUP,)),
            dma((groups,)),
            dma((groups,)),
        ],
        compiler_params=pltpu.CompilerParams(
            collective_id=0, has_side_effects=True, vmem_limit_bytes=48 * 1024 * 1024
        ),
    )(
        forcing,
        kappa.reshape(1, ROWS),
        elem_order,
        *[jnp.asarray(table, F32) for table in tables],
    )


def solution(mesh):
    in_specs = (P(("elem", "face"), None), P(("elem", "face")), P(("elem", "face"), None))
    out_specs = (P(("elem", "face"), None), P(("elem", "face"), None))
    size = mesh.shape["elem"] * mesh.shape["face"]
    return jax.shard_map(
        functools.partial(per_device, size),
        mesh=mesh,
        in_specs=in_specs,
        out_specs=out_specs,
        check_vma=False,
    )
```

time: 636 us -> 44.3 us (0.07); the launches traced: 625 us -> 44 us
  local copies, waits for them, and re-layouts: 252 us -> 7.45 us
  blocking collectives: 211 us -> 0 us
  starting transfers between devices: 75.4 us -> 0 us
  other arithmetic: 37.6 us -> 0 us
  Pallas kernels: 0 us -> 35.8 us
  waiting for transfers between devices: 30.9 us -> 0 us
  matrix products: 10.5 us -> 0 us
  between operations: 7.45 us -> 0.66 us
    psum x3 -> x0, blocking collectives: 211 us -> none  [the longest x2 139 us: progress(): return lax.psum(inner(resid, precond), ('elem', 'face'))]
    slice x191 -> x0, local copies, waits for them, and re-layouts: 95.9 us -> none  [the longest x7 37.8 us: pair_sum(): middle = lax.slice_in_dim(grid, 1, 7, axis=node_axis)]
    ppermute x27 -> x0, starting transfers between devices: 75.4 us -> none  [the longest x19 64.7 us: from_behind(): return lax.ppermute(x, axis, [(i, (i + by) % size) for i in range(size)])]
    reshape x16 -> x0, local copies, waits for them, and re-layouts: 51.9 us -> none  [the longest x4 29 us: direct_sum(): return grid.reshape(-1, 512)]
    unnamed x228 -> x18, local copies, waits for them, and re-layouts: 50.6 us -> 7.45 us
    concatenate x142 -> x0, local copies, waits for them, and re-layouts: 37.4 us -> none  [the longest x4 31.1 us: direct_sum(): jnp.concatenate([first[:, :, :, None], grid[:, :, :, 1:7], shared[:, :, :...]
    pallas_call x0 -> x1, Pallas kernels: none -> 35.8 us  [per_device(): pl.pallas_call(functools.partial(kernel, size), out_shape=(field, field),...]
    ppermute x27 -> x0, waiting for transfers between devices: 30.9 us -> none  [the longest x19 21.1 us: from_behind(): return lax.ppermute(x, axis, [(i, (i + by) % size) for i in range(size)])]
  transfers between devices with their start and end apart: 27 -> 0, of which waited for: 17 -> 0; matrix products, arithmetic and copies ran while one was open for 19% -> 0% of each run, Pallas kernels for 0% -> 0%
where the time goes in v1:
time: 44.3 us; the launch traced here: 44 us
  Pallas kernels  35.8 us (81%)
  local copies, waits for them, and re-layouts  7.45 us (17%)
  between operations  0.66 us (1%)
    pallas_call x1, Pallas kernels, per_device(): pl.pallas_call(functools.partial(kernel, size), out_shape=(field, field),...  35.8 us
    unnamed x18, local copies, waits for them, and re-layouts  7.45 us

profile of v1, /device:TPU:1, one launch (start us, length us, event | category | flops | bytes accessed | tf_op | source)
XLA Modules:
  0.0 44.0 jit_solution(5629560526641056186)
XLA Ops:
  0.6 0.0 copy-start.4
  0.6 0.0 copy-start.6
  0.7 0.7 %copy-done.4 = f32[1,512]{1,0:T(1,128)S(1)} copy-done((f32[1,512]{1,0:T(1,128)S(1)}, f32[1,512]{1,0:T(1,128)}, u32[]{:S(2)}) %copy-start.4) | copy-done | bytes 2072
  1.3 0.0 copy-done.6
  1.3 0.0 copy-start
  1.3 1.2 %copy-done = f32[512,512]{1,0:T(8,128)S(1)} copy-done((f32[512,512]{1,0:T(8,128)S(1)}, f32[512,512]{1,0:T(8,128)}, u32[]{:S(2)}) %copy-start) | copy-done | bytes 1048600
  2.6 0.0 copy-start.1
  2.6 1.0 %copy-done.1 = f32[256,512]{1,0:T(8,128)S(1)} copy-done((f32[256,512]{1,0:T(8,128)S(1)}, f32[256,512]{1,0:T(8,128)}, u32[]{:S(2)}) %copy-start.1) | copy-done | bytes 524312
  3.6 0.0 copy-start.2
  3.6 0.8 %copy-done.2 = f32[32,512]{1,0:T(8,128)S(1)} copy-done((f32[32,512]{1,0:T(8,128)S(1)}, f32[32,512]{1,0:T(8,128)}, u32[]{:S(2)}) %copy-start.2) | copy-done | bytes 65560
  4.4 0.0 copy-start.3
  4.4 0.7 %copy-done.3 = f32[8,512]{1,0:T(8,128)S(1)} copy-done((f32[8,512]{1,0:T(8,128)S(1)}, f32[8,512]{1,0:T(8,128)}, u32[]{:S(2)}) %copy-start.3) | copy-done | bytes 16408
  5.2 0.0 copy-start.5
  5.2 0.7 %copy-done.5 = f32[1,512]{1,0:T(1,128)S(1)} copy-done((f32[1,512]{1,0:T(1,128)S(1)}, f32[1,512]{1,0:T(1,128)}, u32[]{:S(2)}) %copy-start.5) | copy-done | bytes 2072
  5.8 0.0 copy-start.7
  5.8 0.7 %copy-done.7 = s32[1,256]{1,0:T(1,128)S(1)} copy-done((s32[1,256]{1,0:T(1,128)S(1)}, s32[1,256]{1,0:T(1,128)}, u32[]{:S(2)}) %copy-start.7) | copy-done | bytes 1048
  6.5 35.8 %shard_map.95 = (f32[256,512]{1,0:T(8,128)S(1)}, f32[256,512]{1,0:T(8,128)S(1)}) custom-call(f32[256,512]{1,0:T(8,128)S(1)} %copy-done.1, f32[1,256]{1,0:T(1,128)S(1)} %bitcast.1, s32[1,256]{1,0:T(1,128)S(1)} %copy-done.7, f32[512,512]{1,0:T(8,128)S(1)} %copy-done, f32[1,512]{1,0:T(1,128)S(1)} %copy-done.5, f32[8,512]{1,0:T(8,128)S(1)} %copy-done.3, ...), custom_call_target="tpu_custom_call" | custom-call | tf_op jit(solution)/shard_map/pallas_call | solution.py:469
  42.4 0.8 %copy.12 = f32[256,512]{1,0:T(8,128)} copy(f32[256,512]{1,0:T(8,128)S(1)} %get-tuple-element.4) | data formatting | bytes 1048576
  43.2 0.8 %copy.13 = f32[256,512]{1,0:T(8,128)} copy(f32[256,512]{1,0:T(8,128)S(1)} %get-tuple-element.5) | data formatting | bytes 1048576
Async XLA Ops:
  0.6 0.7 %copy-start.4 = (f32[1,512]{1,0:T(1,128)S(1)}, f32[1,512]{1,0:T(1,128)}, u32[]{:S(2)}) copy-start(f32[1,512]{1,0:T(1,128)} %constant.14.clone.fixed_ref) | copy-start | bytes 6148
  0.6 0.7 %copy-start.6 = (f32[256]{0:T(256)S(1)}, f32[256]{0:T(256)}, u32[]{:S(2)}) copy-start(f32[256]{0:T(256)} %param.9) | copy-start | bytes 3076
  1.3 1.2 %copy-start = (f32[512,512]{1,0:T(8,128)S(1)}, f32[512,512]{1,0:T(8,128)}, u32[]{:S(2)}) copy-start(f32[512,512]{1,0:T(8,128)} %constant.10.clone.stiff_ref) | copy-start | bytes 3145732
  2.6 1.0 %copy-start.1 = (f32[256,512]{1,0:T(8,128)S(1)}, f32[256,512]{1,0:T(8,128)}, u32[]{:S(2)}) copy-start(f32[256,512]{1,0:T(8,128)} %forcing_ref.1) | copy-start | bytes 1572868
  3.6 0.8 %copy-start.2 = (f32[32,512]{1,0:T(8,128)S(1)}, f32[32,512]{1,0:T(8,128)}, u32[]{:S(2)}) copy-start(f32[32,512]{1,0:T(8,128)} %constant.13.clone.share_ref) | copy-start | bytes 196612
  4.4 0.7 %copy-start.3 = (f32[8,512]{1,0:T(8,128)S(1)}, f32[8,512]{1,0:T(8,128)}, u32[]{:S(2)}) copy-start(f32[8,512]{1,0:T(8,128)} %constant.12.clone.prolong_ref) | copy-start | bytes 49156
  5.2 0.7 %copy-start.5 = (f32[1,512]{1,0:T(1,128)S(1)}, f32[1,512]{1,0:T(1,128)}, u32[]{:S(2)}) copy-start(f32[1,512]{1,0:T(1,128)} %constant.11.clone.mass_ref) | copy-start | bytes 6148
  5.8 0.7 %copy-start.7 = (s32[1,256]{1,0:T(1,128)S(1)}, s32[1,256]{1,0:T(1,128)}, u32[]{:S(2)}) copy-start(s32[1,256]{1,0:T(1,128)} %order_ref.1) | copy-start | bytes 3076

commit v2 on v0

v2 whole, which is shorter than its diff:
```python
import functools

import jax
import jax.numpy as jnp
import numpy as np
from jax import lax
from jax.experimental import pallas as pl
from jax.experimental.pallas import tpu as pltpu
from jax.sharding import PartitionSpec as P

EX = 8
EY = 32
ROWS = EX * EY
NODES = 512
REACT = 0.02
OMEGA = 0.6
REACH = 8
NEAR = 4
PIECES = ((0, 0), (0, 1), (0, 2), (1, 0), (1, 1), (2, 0))
MESH = pl.DeviceIdType.MESH
F32 = jnp.float32
BF16 = jnp.bfloat16


def legendre_seven(points):
    before = np.ones(8)
    current = np.array(points)
    for degree in range(1, 7):
        following = ((2 * degree + 1) * points * current - degree * before) / (degree + 1)
        before = current
        current = following
    return current


def element_tables():
    points = np.array(
        [
            -1.0,
            -0.8717401485096066,
            -0.5917001814331423,
            -0.2092992179024789,
            0.2092992179024789,
            0.5917001814331423,
            0.8717401485096066,
            1.0,
        ]
    )
    weights = np.array(
        [
            1.0 / 28.0,
            0.2107042271435061,
            0.3411226924835044,
            0.4124587946587038,
            0.4124587946587038,
            0.3411226924835044,
            0.2107042271435061,
            1.0 / 28.0,
        ]
    )
    legendre = legendre_seven(points)
    derivative = np.zeros((8, 8))
    for left_node in range(8):
        for right_node in range(8):
            if left_node != right_node:
                derivative[left_node, right_node] = legendre[left_node] / (
                    legendre[right_node] * (points[left_node] - points[right_node])
                )
    derivative[0, 0] = -14.0
    derivative[7, 7] = 14.0
    stiffness = derivative.T @ (weights[:, None] * derivative)
    mass = np.eye(8) * weights[None, :]
    full_stiff = (
        np.kron(np.kron(mass, mass), stiffness)
        + np.kron(np.kron(mass, stiffness), mass)
        + np.kron(np.kron(stiffness, mass), mass)
    )
    mass_nodes = np.kron(np.kron(weights, weights), weights)
    interp = np.stack([(1.0 - points) / 2.0, (1.0 + points) / 2.0], 1)
    prolong = np.kron(np.kron(interp, interp), interp)
    return full_stiff, mass_nodes, prolong


def pieces_of(table, count):
    parts = []
    for _ in range(count):
        part = table.astype(BF16).astype(np.float64)
        parts.append(part)
        table = table - part
    return parts


def ends(offset):
    if offset == 0:
        return list(range(8)), list(range(8))
    return ([7], [0]) if offset == 1 else ([0], [7])


def all_tables():
    full_stiff, mass_nodes, prolong = element_tables()
    face = np.concatenate([np.arange(64), np.arange(448, 512)])
    facing = np.concatenate([np.arange(448, 512), np.arange(64)])
    diag = np.diag(full_stiff).reshape(8, 8, 8)
    mass = mass_nodes.reshape(8, 8, 8)
    share = np.zeros((16, 8, 8, 8))
    fixed = np.zeros((8, 8, 8))
    for index in range(9):
        offsets = (0, index // 3 - 1, index % 3 - 1)
        mine = np.ix_(*[ends(offset)[0] for offset in offsets])
        theirs = np.ix_(*[ends(offset)[1] for offset in offsets])
        share[index][mine] += diag[theirs]
        fixed[mine] += REACT * mass[theirs]
    share, fixed = share.reshape(16, NODES), fixed.reshape(NODES)
    fixed_face = 2.0 * fixed[face]
    share_face = np.zeros((48, 128))
    share_face[0:16] = share[:, face]
    share_face[16:32, :64] = share[:, facing[:64]]
    share_face[32:48, 64:] = share[:, facing[64:]]

    steep = full_stiff @ prolong
    heavy = REACT * mass_nodes[:, None] * prolong

    def stacked(table):
        parts = pieces_of(table, 3)
        return np.concatenate([parts[right] for _, right in PIECES], 0)

    spread = stacked(np.concatenate([prolong.T, steep.T], 1))
    facing_tables = np.concatenate([steep[facing].T, heavy[facing].T], 1)
    lower = facing_tables.copy()
    lower[:, 64:128] = 0.0
    lower[:, 192:256] = 0.0
    spread_face = np.concatenate([stacked(lower), stacked(facing_tables - lower)], 0)

    gather = pieces_of(np.concatenate([steep.T, heavy.T], 0), 2)
    gather = np.concatenate(gather, 0)
    first = np.concatenate(pieces_of(prolong.T, 2), 0)
    return {
        "stiff": full_stiff,
        "spread": spread,
        "spread_face": spread_face,
        "gather": np.concatenate([gather, first], 0),
        "share": share,
        "share_face": share_face,
        "rows": np.concatenate(
            [
                np.stack([fixed, REACT * mass_nodes]),
                np.pad(np.stack([fixed_face, REACT * mass_nodes[face]]), ((0, 0), (0, 384))),
            ],
            0,
        ),
    }


def split(value, pieces):
    parts = []
    for _ in range(pieces):
        part = value.astype(BF16)
        parts.append(part)
        value = value - part.astype(F32)
    return parts


def dot(left, right, dims=((1,), (0,))):
    return lax.dot_general(
        left, right, (dims, ((), ())), precision=lax.Precision.HIGHEST, preferred_element_type=F32
    )


def dot16(left, right, dims=((1,), (0,))):
    return lax.dot_general(left, right, (dims, ((), ())), preferred_element_type=F32)


def lanes(shape):
    return lax.broadcasted_iota(jnp.int32, shape, len(shape) - 1)


def roll_x(plane, by):
    size = plane.shape[1]
    along = lanes(plane.shape) % EX
    inside = pltpu.roll(plane, by % size, 1)
    around = pltpu.roll(plane, (by - EX * by) % size, 1)
    return jnp.where(along == (0 if by == 1 else EX - 1), around, inside)


def roll_y(plane, by):
    return pltpu.roll(plane, (by * EX) % plane.shape[1], 1)


def down(plane):
    return pltpu.roll(plane, plane.shape[0] - 1, 0)


def up(plane):
    return pltpu.roll(plane, 1, 0)


def shared_xy(tile):
    cube = tile.reshape(EY, EX, 128)
    lane = lanes(cube.shape)
    nx, ny = lane % 8, lane // 8 % 8
    after = pltpu.roll(pltpu.roll(cube, EX - 1, 1), 7, 2)
    before = pltpu.roll(pltpu.roll(cube, 1, 1), 128 - 7, 2)
    cube = cube + jnp.where(nx == 7, after, jnp.where(nx == 0, before, 0.0))
    after = pltpu.roll(jnp.concatenate([cube[1:], cube[:1]], 0), 56, 2)
    before = pltpu.roll(jnp.concatenate([cube[-1:], cube[:-1]], 0), 128 - 56, 2)
    cube = cube + jnp.where(ny == 7, after, jnp.where(ny == 0, before, 0.0))
    return cube.reshape(ROWS, 128)


def four(layer):
    moved = [layer, roll_x(layer, 1)]
    return moved + [roll_y(moved[0], 1), roll_y(moved[1], 1)]


def nine(layer):
    side = {0: layer, 1: roll_x(layer, -1), -1: roll_x(layer, 1)}
    return [
        side[dx] if dy == 0 else roll_y(side[dx], -dy) for dy in (-1, 0, 1) for dx in (-1, 0, 1)
    ]


def coarse_stencil(layer4, planes):
    found = {}
    for dy in (-1, 0, 1):
        for dx in (-1, 0, 1):
            rows = (0, 1) if dy == 0 else ((0,) if dy == 1 else (1,))
            cols = (0, 1) if dx == 0 else ((0,) if dx == 1 else (1,))
            differ = abs(dy) + abs(dx) + (1 - planes)
            count = len(rows) * len(cols) * (1 + planes)
            weight = REACT * count * 2.0 ** (3 - differ) / 27.0
            if differ >= 2:
                total = sum(layer4[2 * a + b] for a in rows for b in cols)
                found[dy, dx] = (-1.0 / 6.0) * total + weight
            elif differ == 1:
                found[dy, dx] = weight
    return found


def swept(vert, level, from_above, from_below):
    along = {0: vert, 1: roll_x(vert, -1), -1: roll_x(vert, 1)}
    spread = {}
    for dx, value in along.items():
        spread[0, dx] = value
        spread[1, dx] = roll_y(value, -1)
        spread[-1, dx] = roll_y(value, 1)
    total = (1.0 - OMEGA) * vert
    total += sum(level[key] * spread[key] for key in level)
    total += down(sum(from_above[key] * spread[key] for key in from_above))
    total += up(sum(from_below[key] * spread[key] for key in from_below))
    return total


NAMES = (
    "stiff",
    "spread",
    "spread_face",
    "gather",
    "share",
    "share_face",
    "rows",
)
FIELDS = ("load", "r0", "x0", "z0", "q", "qloc", "x1", "y", "w", "inverse", "stiffened")


def kernel(size, *refs):
    refs = list(refs)

    def take(count):
        taken = refs[:count]
        del refs[:count]
        return taken

    sources = take(3 + len(NAMES))
    solution_ref, residual_ref = take(2)
    inputs = take(3 + len(NAMES))
    forcing_ref, kappa_ref, order_ref = inputs[:3]
    table = dict(zip(NAMES, inputs[3:]))
    field = dict(zip(FIELDS, take(len(FIELDS))))
    coeff_ref, sent_z0, sent_q, sent_r0, sent_y, sent_w = take(6)
    stiff_ref, stiff_face_ref = take(2)
    edge_out, edge_in, halo, rest, sums_ref = take(5)
    in_sem, halo_send, halo_recv, rest_send, rest_recv = take(5)
    edge_send, edge_recv, sum_send, sum_recv = take(4)

    me = lax.axis_index("elem") * 2 + lax.axis_index("face")

    def ring(by):
        device = lax.rem(me + by + size, size)
        return lax.div(device, 2), lax.rem(device, 2)

    barrier = pltpu.get_barrier_semaphore()

    def greet(by, carry):
        pl.semaphore_signal(barrier, inc=1, device_id=ring(by), device_id_type=MESH)
        return carry

    loads = [
        pltpu.make_async_copy(source, target, in_sem.at[index])
        for index, (source, target) in enumerate(zip(sources, inputs))
    ]
    for index in (2, 1, 0, *range(len(loads) - 1, 2, -1)):
        loads[index].start()
    lax.fori_loop(1, size, greet, 0)

    def remote(source, target, send, recv, device):
        return pltpu.make_async_remote_copy(
            src_ref=source,
            dst_ref=target,
            send_sem=send,
            recv_sem=recv,
            device_id=device,
            device_id_type=MESH,
        )

    def to_ring(buffer, send, recv, reach):
        found = {}
        for by in sorted(range(-reach, reach + 1), key=abs):
            if by != 0:
                at = reach - by
                found[by] = remote(buffer.at[reach], buffer.at[at], send.at[at], recv.at[at], ring(by))
        return found

    half = lanes((ROWS, 128)) < 64

    def tile(ref, index):
        return ref[:, 128 * index : 128 * index + 128]

    def put(ref, index, value):
        ref[:, 128 * index : 128 * index + 128] = value

    def face_of(ref):
        return jnp.where(half, tile(ref, 0), tile(ref, 3))

    def put_face(ref, value):
        put(ref, 0, jnp.where(half, value, tile(ref, 0)))
        put(ref, 3, jnp.where(half, tile(ref, 3), value))

    def send_faces(face, turn):
        top, bottom, part = face[0:128], face[128:256], half[0:128]
        edge_out[turn, 0] = jnp.where(part, pltpu.roll(top, 64, 1), bottom)
        edge_out[turn, 1] = jnp.where(part, top, pltpu.roll(bottom, 64, 1))
        copies = [
            remote(
                edge_out.at[turn, way],
                edge_in.at[turn, way],
                edge_send.at[turn, way],
                edge_recv.at[turn, way],
                ring(by),
            )
            for way, by in ((0, 1), (1, -1))
        ]
        for copy in copies:
            copy.start()
        return copies

    def faces_arrived(copies, turn):
        for copy in copies:
            copy.wait_recv()
        below, above, part = edge_in[turn, 0], edge_in[turn, 1], half[0:128]
        top = jnp.where(part, below, pltpu.roll(above, 64, 1))
        bottom = jnp.where(part, pltpu.roll(below, 64, 1), above)
        return jnp.concatenate([top, bottom], 0)

    def vertex_sums(each):
        corner = lax.broadcasted_iota(jnp.int32, each.shape, 0)
        each = jnp.where(corner % 2 == 1, roll_x(each, 1), each)
        each = jnp.where(corner // 2 % 2 == 1, roll_y(each, 1), each)
        low = jnp.sum(each[0:4], axis=0, keepdims=True)
        high = jnp.sum(each[4:8], axis=0, keepdims=True)
        return low, high

    def gathered(matrix, parts):
        whole = dot16(matrix, parts[0], ((1,), (1,)))
        return whole[0:16] + whole[16:32] + dot16(matrix[0:16], parts[1], ((1,), (1,)))

    def face_lanes(value):
        return jnp.concatenate([value[:, 0:64], value[:, 448:512]], 1)

    def columns(planes):
        return jnp.concatenate(planes, 0).T

    def corner_pieces(corners):
        parts = [part.astype(F32) for part in split(corners, 3)]
        return [parts[left] for left, _ in PIECES]

    row = lax.broadcasted_iota(jnp.int32, (ROWS, ROWS), 0)
    loads[2].wait()
    pick = jnp.where(row == order_ref[...], 1.0, 0.0)
    pick16 = pick.astype(BF16)
    loads[1].wait()
    kappa_rows = jnp.broadcast_to(kappa_ref[...], (16, ROWS))
    kappa = sum(dot16(part, pick16, ((1,), (1,))) for part in split(kappa_rows, 3))[0:8]
    halo[REACH, 2:3] = kappa[0:1]
    loads[0].wait()
    load_ref, r0_ref = field["load"], field["r0"]
    load_ref[...] = sum(dot16(pick16, part) for part in split(forcing_ref[...], 3))
    put(r0_ref, 0, shared_xy(tile(load_ref, 0)))
    put(r0_ref, 3, shared_xy(tile(load_ref, 3)))
    for copy in loads[3:]:
        copy.wait()
    parts = split(load_ref[...], 2)
    gather = table["gather"][0:32].astype(BF16)
    gather_face = face_lanes(gather)
    first = table["gather"][32:48].astype(BF16)
    each = dot16(first, parts[0], ((1,), (1,)))
    each = each[0:8] + each[8:16] + dot16(first, parts[1], ((1,), (1,)))[0:8]
    low, high = vertex_sums(each)
    halo[REACH, 0:1] = low
    halo[REACH, 1:2] = high
    stiff = table["stiff"][...]
    upper_piece = stiff.astype(BF16)
    stiff_ref[0:NODES] = upper_piece
    stiff_ref[NODES:] = (stiff - upper_piece.astype(F32)).astype(BF16)
    for at, piece in ((0, 0), (128, 0), (256, NODES)):
        stiff_face_ref[at : at + 64] = stiff_ref[piece : piece + 64]
        stiff_face_ref[at + 64 : at + 128] = stiff_ref[piece + 448 : piece + 512]
    stiff_face_face = face_lanes(stiff_face_ref[...])
    spread_table = table["spread"][...].astype(BF16)
    spread_face_table = table["spread_face"][...].astype(BF16)
    pl.semaphore_wait(barrier, size - 1)
    halo_copies = to_ring(halo, halo_send, halo_recv, REACH)
    halo_copies[1].start()
    halo_copies[-1].start()
    edges = [send_faces(face_of(r0_ref), 0)]
    for by, copy in halo_copies.items():
        if abs(by) > 1:
            copy.start()

    put(r0_ref, 1, shared_xy(tile(load_ref, 1)))
    put(r0_ref, 2, shared_xy(tile(load_ref, 2)))
    own9 = nine(kappa)
    own_rows = [plane[0:1] for plane in own9] + [jnp.zeros((7, ROWS), F32)]
    own_columns = columns(own_rows)
    coeff_ref[...] = jnp.broadcast_to(own_columns[:, 4:5], (ROWS, 128))
    fixed, mass = table["rows"][0:1], table["rows"][1:2]
    fixed_face, mass_face = table["rows"][2:3, 0:128], table["rows"][3:4, 0:128]
    field["inverse"][...] = 1.0 / (dot(own_columns, table["share"][...]) + fixed)
    back16 = pick.T.astype(BF16)

    def interior(value, x_ref):
        inverse = field["inverse"]
        zero = jnp.zeros((ROWS, 128), F32)
        put(x_ref, 0, jnp.where(half, zero, tile(inverse, 0) * tile(value, 0)))
        put(x_ref, 1, tile(inverse, 1) * tile(value, 1))
        put(x_ref, 2, tile(inverse, 2) * tile(value, 2))
        put(x_ref, 3, jnp.where(half, tile(inverse, 3) * tile(value, 3), zero))
        parts = split(x_ref[...], 2)
        high, low = stiff_ref[0:NODES], stiff_ref[NODES:]
        field["stiffened"][...] = (
            dot16(parts[0], high) + dot16(parts[1], high) + dot16(parts[0], low)
        )
        return gathered(gather, parts)

    inner_rows = interior(r0_ref, field["x0"])

    for by in (1, -1):
        halo_copies[by].wait_recv()
    below9 = nine(jnp.broadcast_to(halo[REACH - 1, 2:3], (8, ROWS)))
    above9 = nine(jnp.broadcast_to(halo[REACH + 1, 2:3], (8, ROWS)))
    pad = [jnp.zeros((7, ROWS), F32)]
    three = columns(
        own_rows + [p[0:1] for p in below9] + pad + [p[0:1] for p in above9] + pad
    )
    inverse_face = 1.0 / (dot(three, table["share_face"][...]) + fixed_face)
    coeff_beside = jnp.where(half, three[:, 20:21], three[:, 36:37])
    coeff = coeff_ref[...]
    face = face_of(r0_ref) + faces_arrived(edges[0], 0)
    put_face(r0_ref, face)

    def outer(face, x_ref, rows):
        x_face = inverse_face * face
        put_face(x_ref, x_face)
        parts = split(x_face, 2)
        rows = rows + gathered(gather_face, parts)
        return x_face, jnp.concatenate([parts[0], parts[1], parts[0]], 1), rows

    x_face, stacked, rows0 = outer(face, field["x0"], inner_rows)
    rough = coeff * (
        face_of(field["stiffened"]) + dot16(stacked, stiff_face_face)
    ) + mass_face * x_face
    edges.append(send_faces(shared_xy(rough), 1))
    low, high = vertex_sums(kappa * rows0[0:8] + rows0[8:16])
    rest[NEAR, 0:1] = low
    rest[NEAR, 1:2] = high
    rest_copies = to_ring(rest, rest_send, rest_recv, NEAR)
    for copy in rest_copies.values():
        copy.start()

    field["stiffened"][...] += dot16(stacked, stiff_face_ref[...])
    for by, copy in halo_copies.items():
        if abs(by) > 1:
            copy.wait_recv()
    planes = list(range(-3, REACH + 1)) + list(range(1 - REACH, -3))

    def halo_rows(shift, which):
        return jnp.concatenate([halo[REACH + p + shift, which : which + 1] for p in planes], 0)

    under4, over4 = four(halo_rows(-1, 2)), four(halo_rows(0, 2))
    both4 = [a + b for a, b in zip(under4, over4)]
    diag = (2.0 / 3.0) * (both4[0] + both4[1] + both4[2] + both4[3]) + REACT * 64.0 / 27.0
    damp = -OMEGA / diag
    damp_down, damp_up = up(damp), down(damp)
    level = {key: damp * value for key, value in coarse_stencil(both4, 1).items()}
    from_above = {key: damp_down * value for key, value in coarse_stencil(under4, 0).items()}
    from_below = {key: damp_up * value for key, value in coarse_stencil(over4, 0).items()}
    start = -damp * (halo_rows(0, 0) + halo_rows(-1, 1))
    vert = start
    for _ in range(3):
        vert = start + swept(vert, level, from_above, from_below)
    remainder = (vert - swept(vert, level, from_above, from_below))[0:8]

    def corners_of(vert, lower):
        one = roll_x(vert, -1)
        found = [vert, one, roll_y(vert, -1), roll_y(one, -1)]
        return [
            jnp.concatenate(
                [c[k : k + 1] for c in found] + [c[k + 1 : k + 2] for c in found], 0
            )
            for k in lower
        ]

    own, under, over = corners_of(vert[0:8], (3, 2, 4))
    spread = dot16(columns(corner_pieces(own)).astype(BF16), spread_table)
    beside = dot16(
        columns(corner_pieces(under) + corner_pieces(over)).astype(BF16),
        spread_face_table,
    )
    beside = shared_xy(coeff_beside * beside[:, 0:128] + beside[:, 128:256])

    def total(value):
        return jnp.sum(jnp.sum(value.reshape(ROWS // 8, 8, 128), axis=0), axis=(0, 1), keepdims=True)

    def applied(x_ref, spread, z_ref, image_ref):
        for index in range(4):
            at = 128 * index
            z = tile(x_ref, index) + spread[:, at : at + 128]
            put(z_ref, index, z)
            put(
                image_ref,
                index,
                coeff * (tile(field["stiffened"], index) + spread[:, 512 + at : 640 + at])
                + mass[:, at : at + 128] * z,
            )

    def inner(left, right):
        return total(sum(tile(left, index) * tile(right, index) for index in range(4)))

    applied(field["x0"], spread, field["z0"], field["qloc"])
    rz = inner(load_ref, field["z0"])
    zq = inner(field["qloc"], field["z0"])
    for index in range(4):
        put(field["q"], index, shared_xy(tile(field["qloc"], index)))
    partial_face = face_of(field["q"]) + beside
    inner_rows = interior(field["q"], field["x1"])

    face = partial_face + faces_arrived(edges[1], 1)
    put_face(field["q"], face)
    x_face, stacked, _ = outer(face, field["x1"], inner_rows)
    field["stiffened"][...] += dot16(stacked, stiff_face_ref[...])
    for copy in rest_copies.values():
        copy.wait_recv()
    target = jnp.concatenate([rest[NEAR + p, 0:1] for p in range(-3, 5)], 0) + jnp.concatenate(
        [rest[NEAR + p - 1, 1:2] for p in range(-3, 5)], 0
    )

    def top(parts):
        return {key: value[0:8] for key, value in parts.items()}

    level, from_above, from_below = top(level), top(from_above), top(from_below)
    start = remainder - damp[0:8] * target
    vert = start
    for _ in range(3):
        vert = start + swept(vert, level, from_above, from_below)
    (own,) = corners_of(vert, (3,))
    spread = dot16(columns(corner_pieces(own)).astype(BF16), spread_table)
    applied(field["x1"], spread, field["y"], field["w"])
    qy = inner(field["qloc"], field["y"])
    yw = inner(field["w"], field["y"])

    lane = lanes((1, 128))
    mine = jnp.zeros((1, 128), F32)
    for index, value in enumerate((rz, zq, qy, yw)):
        mine = jnp.where(lane == index, value, mine)
    sums_ref[0] = mine

    def spread_sums(by, carry):
        remote(sums_ref.at[0], sums_ref.at[by], sum_send, sum_recv, ring(by)).start()
        return carry

    lax.fori_loop(1, size, spread_sums, 0)
    put(field["w"], 0, shared_xy(tile(field["w"], 0)))
    put(field["w"], 3, shared_xy(tile(field["w"], 3)))
    edges.append(send_faces(face_of(field["w"]), 2))
    put(field["w"], 1, shared_xy(tile(field["w"], 1)))
    put(field["w"], 2, shared_xy(tile(field["w"], 2)))

    def stored(value):
        return sum(dot16(back16, part) for part in split(value, 3))

    sent_z0[...] = stored(field["z0"][...])
    sent_y[...] = stored(field["y"][...])
    sent_r0[...] = stored(r0_ref[...])
    sent_q[...] = stored(field["q"][...])
    face = face_of(field["w"]) + faces_arrived(edges[2], 2)
    put_face(field["w"], face)
    sent_w[...] = stored(field["w"][...])
    others = sums_ref.at[pl.ds(1, size - 1)]
    all_sums = remote(others, others, sum_send, sum_recv, ring(1))
    all_sums.wait_recv()
    sums = jnp.sum(sums_ref[...], axis=0)
    rz, zq, qy, yw = (sums[:, index : index + 1] for index in range(4))
    first = rz / zq
    gamma = first * first * qy - rz
    grown = 1.0 + gamma / rz
    second = gamma / (grown * grown * zq - 2.0 * first * grown * qy + first * first * yw)
    straight, bent = first + second * grown, first * second
    solution_ref[...] = straight * sent_z0[...] - bent * sent_y[...]
    residual_ref[...] = sent_r0[...] - straight * sent_q[...] + bent * sent_w[...]

    all_sums.wait_send()
    for copies in [halo_copies.values(), rest_copies.values()] + edges:
        for copy in copies:
            copy.wait_send()


def per_device(size, forcing, kappa, elem_order):
    tables = all_tables()
    operands = [forcing, kappa.reshape(1, ROWS), elem_order]
    operands += [jnp.asarray(tables[name], F32) for name in NAMES]
    out = jax.ShapeDtypeStruct((ROWS, NODES), F32)
    count, close = 2 * REACH + 1, 2 * NEAR + 1
    dma = pltpu.SemaphoreType.DMA
    return pl.pallas_call(
        functools.partial(kernel, size),
        out_shape=(out, out),
        in_specs=[pl.BlockSpec(memory_space=pl.ANY)] * len(operands),
        out_specs=(pl.BlockSpec(memory_space=pltpu.VMEM),) * 2,
        scratch_shapes=[pltpu.VMEM(operand.shape, operand.dtype) for operand in operands]
        + [pltpu.VMEM((ROWS, NODES), F32)] * len(FIELDS)
        + [pltpu.VMEM((ROWS, 128), F32)]
        + [pltpu.VMEM((ROWS, NODES), F32)] * 5
        + [pltpu.VMEM((2 * NODES, NODES), BF16), pltpu.VMEM((384, NODES), BF16)]
        + [
            pltpu.VMEM((3, 2, 128, 128), F32),
            pltpu.VMEM((3, 2, 128, 128), F32),
            pltpu.VMEM((count, 3, ROWS), F32),
            pltpu.VMEM((close, 2, ROWS), F32),
            pltpu.VMEM((size, 1, 128), F32),
            dma((len(operands),)),
            dma((count,)),
            dma((count,)),
            dma((close,)),
            dma((close,)),
            dma((3, 2)),
            dma((3, 2)),
            dma,
            dma,
        ],
        compiler_params=pltpu.CompilerParams(
            collective_id=0, has_side_effects=True, vmem_limit_bytes=56 * 1024 * 1024
        ),
    )(*operands)


def solution(mesh):
    in_specs = (P(("elem", "face"), None), P(("elem", "face")), P(("elem", "face"), None))
    out_specs = (P(("elem", "face"), None), P(("elem", "face"), None))
    size = mesh.shape["elem"] * mesh.shape["face"]
    return jax.shard_map(
        functools.partial(per_device, size),
        mesh=mesh,
        in_specs=in_specs,
        out_specs=out_specs,
        check_vma=False,
    )
```

time: 636 us -> 35.1 us (0.06); the launches traced: 625 us -> 34.4 us
  local copies, waits for them, and re-layouts: 252 us -> 2.72 us
  blocking collectives: 211 us -> 0 us
  starting transfers between devices: 75.4 us -> 0 us
  other arithmetic: 37.6 us -> 0 us
  Pallas kernels: 0 us -> 31.1 us
  waiting for transfers between devices: 30.9 us -> 0 us
  matrix products: 10.5 us -> 0 us
  between operations: 7.45 us -> 0.65 us
    psum x3 -> x0, blocking collectives: 211 us -> none  [the longest x2 139 us: progress(): return lax.psum(inner(resid, precond), ('elem', 'face'))]
    slice x191 -> x0, local copies, waits for them, and re-layouts: 95.9 us -> none  [the longest x7 37.8 us: pair_sum(): middle = lax.slice_in_dim(grid, 1, 7, axis=node_axis)]
    ppermute x27 -> x0, starting transfers between devices: 75.4 us -> none  [the longest x19 64.7 us: from_behind(): return lax.ppermute(x, axis, [(i, (i + by) % size) for i in range(size)])]
    reshape x16 -> x0, local copies, waits for them, and re-layouts: 51.9 us -> none  [the longest x4 29 us: direct_sum(): return grid.reshape(-1, 512)]
    unnamed x228 -> x4, local copies, waits for them, and re-layouts: 50.6 us -> 2.72 us
    concatenate x142 -> x0, local copies, waits for them, and re-layouts: 37.4 us -> none  [the longest x4 31.1 us: direct_sum(): jnp.concatenate([first[:, :, :, None], grid[:, :, :, 1:7], shared[:, :, :...]
    pallas_call x0 -> x1, Pallas kernels: none -> 31.1 us  [per_device(): pl.pallas_call(functools.partial(kernel, size), out_shape=(out, out), in_...]
    ppermute x27 -> x0, waiting for transfers between devices: 30.9 us -> none  [the longest x19 21.1 us: from_behind(): return lax.ppermute(x, axis, [(i, (i + by) % size) for i in range(size)])]
  transfers between devices with their start and end apart: 27 -> 0, of which waited for: 17 -> 0; matrix products, arithmetic and copies ran while one was open for 19% -> 0% of each run, Pallas kernels for 0% -> 0%
where the time goes in v2:
time: 35.1 us; the launch traced here: 34.4 us
  Pallas kernels  31.1 us (89%)
  local copies, waits for them, and re-layouts  2.72 us (8%)
  between operations  0.65 us (2%)
    pallas_call x1, Pallas kernels, per_device(): pl.pallas_call(functools.partial(kernel, size), out_shape=(out, out), in_...  31.1 us
    unnamed x4, local copies, waits for them, and re-layouts  2.72 us

profile of v2, /device:TPU:1, one launch (start us, length us, event | category | flops | bytes accessed | tf_op | source)
XLA Modules:
  0.0 34.4 jit_solution(17199370294514620464)
XLA Ops:
  0.6 31.1 %shard_map.113 = (f32[256,512]{1,0:T(8,128)}, f32[256,512]{1,0:T(8,128)}) custom-call(f32[256,512]{1,0:T(8,128)} %refs_0_.1, f32[1,256]{1,0:T(1,128)} %bitcast.1, s32[1,256]{1,0:T(1,128)} %refs_2_.1, f32[512,512]{1,0:T(8,128)} %constant.14.clone.refs_3_, f32[48,1024]{1,0:T(8,128)} %constant.15.clone.refs_4_, f32[96,256]{1,0:T(8,128)} %constant.16.clone.refs_5_, ...), custom_call_target="tpu_custom_call" | custom-call | tf_op jit(solution)/shard_map/pallas_call | solution.py:632
  31.7 0.0 copy-start
  31.7 1.9 %copy.14 = f32[256,512]{1,0:T(8,128)} copy(f32[256,512]{1,0:T(8,128)} %get-tuple-element.4) | data formatting | bytes 1048576
  33.6 0.0 copy-done
  33.6 0.8 %copy.15 = f32[256,512]{1,0:T(8,128)} copy(f32[256,512]{1,0:T(8,128)S(1)} %copy-done) | data formatting | bytes 1048576
Async XLA Ops:
  31.7 1.9 %copy-start = (f32[256,512]{1,0:T(8,128)S(1)}, f32[256,512]{1,0:T(8,128)}, u32[]{:S(2)}) copy-start(f32[256,512]{1,0:T(8,128)} %get-tuple-element.5) | copy-start | bytes 1572868

commit v3 on v2

--- a/solution.py
+++ b/solution.py
@@ -16,6 +16,7 @@
 OMEGA = 0.6
 REACH = 8
 NEAR = 4
+PARTS = 4
 PIECES = ((0, 0), (0, 1), (0, 2), (1, 0), (1, 1), (2, 0))
 MESH = pl.DeviceIdType.MESH
 F32 = jnp.float32
@@ -270,16 +271,15 @@
         return taken
 
     sources = take(3 + len(NAMES))
-    solution_ref, residual_ref = take(2)
+    sent_z0, sent_y, sent_r0, sent_q, sent_w, steps_ref = take(6)
     inputs = take(3 + len(NAMES))
     forcing_ref, kappa_ref, order_ref = inputs[:3]
     table = dict(zip(NAMES, inputs[3:]))
     field = dict(zip(FIELDS, take(len(FIELDS))))
-    coeff_ref, sent_z0, sent_q, sent_r0, sent_y, sent_w = take(6)
-    stiff_ref, stiff_face_ref = take(2)
-    edge_out, edge_in, halo, rest, sums_ref = take(5)
-    in_sem, halo_send, halo_recv, rest_send, rest_recv = take(5)
-    edge_send, edge_recv, sum_send, sum_recv = take(4)
+    coeff_ref, stiff_ref, stiff_face_ref = take(3)
+    edge_out, edge_in, layer, halo, rest, sums_ref = take(6)
+    in_sem, layer_send, layer_recv, halo_send, halo_recv = take(5)
+    rest_send, rest_recv, edge_send, edge_recv, sum_send, sum_recv, known_sem = take(7)
 
     me = lax.axis_index("elem") * 2 + lax.axis_index("face")
 
@@ -288,10 +288,6 @@
         return lax.div(device, 2), lax.rem(device, 2)
 
     barrier = pltpu.get_barrier_semaphore()
-
-    def greet(by, carry):
-        pl.semaphore_signal(barrier, inc=1, device_id=ring(by), device_id_type=MESH)
-        return carry
 
     loads = [
         pltpu.make_async_copy(source, target, in_sem.at[index])
@@ -299,7 +295,25 @@
     ]
     for index in (2, 1, 0, *range(len(loads) - 1, 2, -1)):
         loads[index].start()
-    lax.fori_loop(1, size, greet, 0)
+    greeted = [by for by in range(-REACH, REACH + 1) if by != 0]
+    for by in greeted:
+        pl.semaphore_signal(barrier, inc=1, device_id=ring(by), device_id_type=MESH)
+
+    stages = []
+    while REACH << len(stages) < size // 2:
+        stages.append(REACH << len(stages))
+
+    def tell(stage):
+        if stage < len(stages):
+            for way, by in enumerate((stages[stage], -stages[stage])):
+                pl.semaphore_signal(
+                    known_sem.at[stage, way], inc=1, device_id=ring(by), device_id_type=MESH
+                )
+
+    def hear(stage):
+        if stage < len(stages):
+            for way in range(2):
+                pl.semaphore_wait(known_sem.at[stage, way], 1)
 
     def remote(source, target, send, recv, device):
         return pltpu.make_async_remote_copy(
@@ -389,44 +403,42 @@
     loads[1].wait()
     kappa_rows = jnp.broadcast_to(kappa_ref[...], (16, ROWS))
     kappa = sum(dot16(part, pick16, ((1,), (1,))) for part in split(kappa_rows, 3))[0:8]
+    layer[1] = kappa[0:1]
     halo[REACH, 2:3] = kappa[0:1]
     loads[0].wait()
     load_ref, r0_ref = field["load"], field["r0"]
-    load_ref[...] = sum(dot16(pick16, part) for part in split(forcing_ref[...], 3))
-    put(r0_ref, 0, shared_xy(tile(load_ref, 0)))
-    put(r0_ref, 3, shared_xy(tile(load_ref, 3)))
+
+    def permuted(matrix, value):
+        return sum(dot16(matrix, part) for part in split(value, 3))
+
+    for index in (0, 3):
+        put(load_ref, index, permuted(pick16, tile(forcing_ref, index)))
+        put(r0_ref, index, shared_xy(tile(load_ref, index)))
+    first_face = face_of(r0_ref)
+    pl.semaphore_wait(barrier, len(greeted))
+    layer_copies = [
+        remote(layer.at[1], layer.at[1 - by], layer_send.at[1 - by], layer_recv.at[1 - by], ring(by))
+        for by in (1, -1)
+    ]
+    for copy in layer_copies:
+        copy.start()
+    edges = [send_faces(first_face, 0)]
+    tell(0)
+
+    for index in (1, 2):
+        put(load_ref, index, permuted(pick16, tile(forcing_ref, index)))
     for copy in loads[3:]:
         copy.wait()
     parts = split(load_ref[...], 2)
-    gather = table["gather"][0:32].astype(BF16)
-    gather_face = face_lanes(gather)
     first = table["gather"][32:48].astype(BF16)
     each = dot16(first, parts[0], ((1,), (1,)))
     each = each[0:8] + each[8:16] + dot16(first, parts[1], ((1,), (1,)))[0:8]
     low, high = vertex_sums(each)
     halo[REACH, 0:1] = low
     halo[REACH, 1:2] = high
-    stiff = table["stiff"][...]
-    upper_piece = stiff.astype(BF16)
-    stiff_ref[0:NODES] = upper_piece
-    stiff_ref[NODES:] = (stiff - upper_piece.astype(F32)).astype(BF16)
-    for at, piece in ((0, 0), (128, 0), (256, NODES)):
-        stiff_face_ref[at : at + 64] = stiff_ref[piece : piece + 64]
-        stiff_face_ref[at + 64 : at + 128] = stiff_ref[piece + 448 : piece + 512]
-    stiff_face_face = face_lanes(stiff_face_ref[...])
-    spread_table = table["spread"][...].astype(BF16)
-    spread_face_table = table["spread_face"][...].astype(BF16)
-    pl.semaphore_wait(barrier, size - 1)
     halo_copies = to_ring(halo, halo_send, halo_recv, REACH)
-    halo_copies[1].start()
-    halo_copies[-1].start()
-    edges = [send_faces(face_of(r0_ref), 0)]
-    for by, copy in halo_copies.items():
-        if abs(by) > 1:
-            copy.start()
-
-    put(r0_ref, 1, shared_xy(tile(load_ref, 1)))
-    put(r0_ref, 2, shared_xy(tile(load_ref, 2)))
+    for copy in halo_copies.values():
+        copy.start()
     own9 = nine(kappa)
     own_rows = [plane[0:1] for plane in own9] + [jnp.zeros((7, ROWS), F32)]
     own_columns = columns(own_rows)
@@ -434,7 +446,14 @@
     fixed, mass = table["rows"][0:1], table["rows"][1:2]
     fixed_face, mass_face = table["rows"][2:3, 0:128], table["rows"][3:4, 0:128]
     field["inverse"][...] = 1.0 / (dot(own_columns, table["share"][...]) + fixed)
-    back16 = pick.T.astype(BF16)
+    stiff = table["stiff"][...]
+    upper_piece = stiff.astype(BF16)
+    stiff_ref[0:NODES] = upper_piece
+    stiff_ref[NODES:] = (stiff - upper_piece.astype(F32)).astype(BF16)
+    put(r0_ref, 1, shared_xy(tile(load_ref, 1)))
+    put(r0_ref, 2, shared_xy(tile(load_ref, 2)))
+    gather = table["gather"][0:32].astype(BF16)
+    gather_face = face_lanes(gather)
 
     def interior(value, x_ref):
         inverse = field["inverse"]
@@ -451,11 +470,15 @@
         return gathered(gather, parts)
 
     inner_rows = interior(r0_ref, field["x0"])
-
-    for by in (1, -1):
-        halo_copies[by].wait_recv()
-    below9 = nine(jnp.broadcast_to(halo[REACH - 1, 2:3], (8, ROWS)))
-    above9 = nine(jnp.broadcast_to(halo[REACH + 1, 2:3], (8, ROWS)))
+    for at, piece in ((0, 0), (128, 0), (256, NODES)):
+        stiff_face_ref[at : at + 64] = stiff_ref[piece : piece + 64]
+        stiff_face_ref[at + 64 : at + 128] = stiff_ref[piece + 448 : piece + 512]
+    stiff_face_face = face_lanes(stiff_face_ref[...])
+
+    for copy in layer_copies:
+        copy.wait_recv()
+    below9 = nine(jnp.broadcast_to(layer[0], (8, ROWS)))
+    above9 = nine(jnp.broadcast_to(layer[2], (8, ROWS)))
     pad = [jnp.zeros((7, ROWS), F32)]
     three = columns(
         own_rows + [p[0:1] for p in below9] + pad + [p[0:1] for p in above9] + pad
@@ -463,7 +486,7 @@
     inverse_face = 1.0 / (dot(three, table["share_face"][...]) + fixed_face)
     coeff_beside = jnp.where(half, three[:, 20:21], three[:, 36:37])
     coeff = coeff_ref[...]
-    face = face_of(r0_ref) + faces_arrived(edges[0], 0)
+    face = first_face + faces_arrived(edges[0], 0)
     put_face(r0_ref, face)
 
     def outer(face, x_ref, rows):
@@ -485,10 +508,13 @@
     for copy in rest_copies.values():
         copy.start()
 
+    hear(0)
+    tell(1)
     field["stiffened"][...] += dot16(stacked, stiff_face_ref[...])
-    for by, copy in halo_copies.items():
-        if abs(by) > 1:
-            copy.wait_recv()
+    spread_table = table["spread"][...].astype(BF16)
+    spread_face_table = table["spread_face"][...].astype(BF16)
+    for copy in halo_copies.values():
+        copy.wait_recv()
     planes = list(range(-3, REACH + 1)) + list(range(1 - REACH, -3))
 
     def halo_rows(shift, which):
@@ -552,9 +578,21 @@
     partial_face = face_of(field["q"]) + beside
     inner_rows = interior(field["q"], field["x1"])
 
+    face_image = face_of(field["qloc"])
+    zero = jnp.zeros((ROWS, 128), F32)
+    qy = inner(field["qloc"], field["x1"])
+    hear(1)
+    tell(2)
+    back16 = pick.T.astype(BF16)
+
+    def stored(value):
+        return permuted(back16, value)
+
+    sent_z0[...] = stored(field["z0"][...])
+    sent_r0[...] = stored(r0_ref[...])
+
     face = partial_face + faces_arrived(edges[1], 1)
-    put_face(field["q"], face)
-    x_face, stacked, _ = outer(face, field["x1"], inner_rows)
+    x_face, stacked, rows1 = outer(face, field["x1"], inner_rows)
     field["stiffened"][...] += dot16(stacked, stiff_face_ref[...])
     for copy in rest_copies.values():
         copy.wait_recv()
@@ -571,11 +609,32 @@
     for _ in range(3):
         vert = start + swept(vert, level, from_above, from_below)
     (own,) = corners_of(vert, (3,))
-    spread = dot16(columns(corner_pieces(own)).astype(BF16), spread_table)
-    applied(field["x1"], spread, field["y"], field["w"])
-    qy = inner(field["qloc"], field["y"])
-    yw = inner(field["w"], field["y"])
-
+
+    def flipped(value, bit):
+        corner = lax.broadcasted_iota(jnp.int32, value.shape, 0)
+        return jnp.where(
+            corner // bit % 2 == 0, pltpu.roll(value, 8 - bit, 0), pltpu.roll(value, bit, 0)
+        )
+
+    edge_sum = flipped(own, 1) + flipped(own, 2) + flipped(own, 4)
+    all_sum = jnp.sum(own, axis=0, keepdims=True)
+    weighed = own
+    for bit in (1, 2, 4):
+        weighed = (2.0 * weighed + flipped(weighed, bit)) * (1.0 / 3.0)
+    steep = (5.0 / 6.0) * own + (1.0 / 6.0) * (edge_sum - all_sum)
+    energy = own * (
+        kappa * (steep + 2.0 * rows1[0:8]) + (REACT * weighed + 2.0 * rows1[8:16])
+    )
+    qy = qy + total(face_image * x_face) + jnp.sum((start * vert / -damp[0:8])[3:4], keepdims=True)
+    yw = jnp.sum(energy, keepdims=True)
+    image = [
+        coeff * tile(field["stiffened"], index)
+        + mass[:, 128 * index : 128 * index + 128] * tile(field["x1"], index)
+        for index in range(4)
+    ]
+    yw = yw + total(sum(image[index] * tile(field["x1"], index) for index in range(4)))
+
+    hear(2)
     lane = lanes((1, 128))
     mine = jnp.zeros((1, 128), F32)
     for index, value in enumerate((rz, zq, qy, yw)):
@@ -587,22 +646,21 @@
         return carry
 
     lax.fori_loop(1, size, spread_sums, 0)
+
+    spread = dot16(columns(corner_pieces(own)).astype(BF16), spread_table)
+    applied(field["x1"], spread, field["y"], field["w"])
     put(field["w"], 0, shared_xy(tile(field["w"], 0)))
     put(field["w"], 3, shared_xy(tile(field["w"], 3)))
     edges.append(send_faces(face_of(field["w"]), 2))
     put(field["w"], 1, shared_xy(tile(field["w"], 1)))
     put(field["w"], 2, shared_xy(tile(field["w"], 2)))
-
-    def stored(value):
-        return sum(dot16(back16, part) for part in split(value, 3))
-
-    sent_z0[...] = stored(field["z0"][...])
+    put_face(field["q"], face)
     sent_y[...] = stored(field["y"][...])
-    sent_r0[...] = stored(r0_ref[...])
     sent_q[...] = stored(field["q"][...])
-    face = face_of(field["w"]) + faces_arrived(edges[2], 2)
-    put_face(field["w"], face)
     sent_w[...] = stored(field["w"][...])
+    face = stored(faces_arrived(edges[2], 2))
+    sent_w[:, 0:128] += jnp.where(half, face, zero)
+    sent_w[:, 384:512] += jnp.where(half, zero, face)
     others = sums_ref.at[pl.ds(1, size - 1)]
     all_sums = remote(others, others, sum_send, sum_recv, ring(1))
     all_sums.wait_recv()
@@ -613,13 +671,33 @@
     grown = 1.0 + gamma / rz
     second = gamma / (grown * grown * zq - 2.0 * first * grown * qy + first * first * yw)
     straight, bent = first + second * grown, first * second
-    solution_ref[...] = straight * sent_z0[...] - bent * sent_y[...]
-    residual_ref[...] = sent_r0[...] - straight * sent_q[...] + bent * sent_w[...]
+    steps_ref[0:1] = jnp.broadcast_to(straight, (1, 128))
+    steps_ref[1:2] = jnp.broadcast_to(bent, (1, 128))
 
     all_sums.wait_send()
-    for copies in [halo_copies.values(), rest_copies.values()] + edges:
+    for copies in [layer_copies, halo_copies.values(), rest_copies.values()] + edges:
         for copy in copies:
             copy.wait_send()
+
+
+def combine(z0, y, r0, q, w, steps, solution_ref, residual_ref, solution_part, residual_part, sem):
+    straight, bent = steps[0:1, 0:1], steps[1:2, 0:1]
+    copies = []
+    rows = ROWS // PARTS
+    for part in range(PARTS):
+        at = pl.ds(part * rows, rows)
+        solution_part[at] = straight * z0[at] - bent * y[at]
+        copies.append(
+            pltpu.make_async_copy(solution_part.at[at], solution_ref.at[at], sem.at[0, part])
+        )
+        copies[-1].start()
+        residual_part[at] = r0[at] - straight * q[at] + bent * w[at]
+        copies.append(
+            pltpu.make_async_copy(residual_part.at[at], residual_ref.at[at], sem.at[1, part])
+        )
+        copies[-1].start()
+    for copy in copies:
+        copy.wait()
 
 
 def per_device(size, forcing, kappa, elem_order):
@@ -627,25 +705,31 @@
     operands = [forcing, kappa.reshape(1, ROWS), elem_order]
     operands += [jnp.asarray(tables[name], F32) for name in NAMES]
     out = jax.ShapeDtypeStruct((ROWS, NODES), F32)
+    steps = jax.ShapeDtypeStruct((8, 128), F32)
     count, close = 2 * REACH + 1, 2 * NEAR + 1
     dma = pltpu.SemaphoreType.DMA
-    return pl.pallas_call(
+    vmem = pl.BlockSpec(memory_space=pltpu.VMEM)
+    hbm = pl.BlockSpec(memory_space=pltpu.HBM)
+    stored = pl.pallas_call(
         functools.partial(kernel, size),
-        out_shape=(out, out),
-        in_specs=[pl.BlockSpec(memory_space=pl.ANY)] * len(operands),
-        out_specs=(pl.BlockSpec(memory_space=pltpu.VMEM),) * 2,
+        out_shape=(out,) * 5 + (steps,),
+        in_specs=[hbm] * len(operands),
+        out_specs=(vmem,) * 6,
         scratch_shapes=[pltpu.VMEM(operand.shape, operand.dtype) for operand in operands]
         + [pltpu.VMEM((ROWS, NODES), F32)] * len(FIELDS)
-        + [pltpu.VMEM((ROWS, 128), F32)]
-        + [pltpu.VMEM((ROWS, NODES), F32)] * 5
-        + [pltpu.VMEM((2 * NODES, NODES), BF16), pltpu.VMEM((384, NODES), BF16)]
         + [
+            pltpu.VMEM((ROWS, 128), F32),
+            pltpu.VMEM((2 * NODES, NODES), BF16),
+            pltpu.VMEM((384, NODES), BF16),
             pltpu.VMEM((3, 2, 128, 128), F32),
             pltpu.VMEM((3, 2, 128, 128), F32),
+            pltpu.VMEM((3, 1, ROWS), F32),
             pltpu.VMEM((count, 3, ROWS), F32),
             pltpu.VMEM((close, 2, ROWS), F32),
             pltpu.VMEM((size, 1, 128), F32),
             dma((len(operands),)),
+            dma((3,)),
+            dma((3,)),
             dma((count,)),
             dma((count,)),
             dma((close,)),
@@ -654,11 +738,26 @@
             dma((3, 2)),
             dma,
             dma,
+            pltpu.SemaphoreType.REGULAR((3, 2)),
         ],
         compiler_params=pltpu.CompilerParams(
-            collective_id=0, has_side_effects=True, vmem_limit_bytes=56 * 1024 * 1024
+            collective_id=0, has_side_effects=True, vmem_limit_bytes=32 * 1024 * 1024
         ),
-    )(*operands)
+        name="solve",
+    )(*[pltpu.with_memory_space_constraint(operand, pltpu.HBM) for operand in operands])
+    return pl.pallas_call(
+        combine,
+        out_shape=(out, out),
+        in_specs=[vmem] * 6,
+        out_specs=(hbm, hbm),
+        scratch_shapes=[
+            pltpu.VMEM((ROWS, NODES), F32),
+            pltpu.VMEM((ROWS, NODES), F32),
+            dma((2, PARTS)),
+        ],
+        compiler_params=pltpu.CompilerParams(vmem_limit_bytes=16 * 1024 * 1024),
+        name="combine",
+    )(*stored)
 
 
 def solution(mesh):

time: 35.1 us -> 31.9 us (0.909)
  local copies, waits for them, and re-layouts: 2.72 us -> 0 us
    unnamed x4 -> x0, local copies, waits for them, and re-layouts: 2.72 us -> none
    pallas_call x1 -> x2, Pallas kernels: 31.1 us -> 30.9 us  [the longest x1 29.8 us: per_device(): pl.pallas_call(functools.partial(kernel, size), out_shape=(out,) * 5 + (s...]
where the time goes in v3:
time: 31.9 us; the launch traced here: 31.5 us
  Pallas kernels  30.9 us (97%)
  between operations  0.64 us (2%)
    pallas_call x1, Pallas kernels, per_device(): pl.pallas_call(functools.partial(kernel, size), out_shape=(out,) * 5 + (s...  29.8 us
    pallas_call x1, Pallas kernels, per_device(): pl.pallas_call(combine, out_shape=(out, out), in_specs=[vmem] * 6, out_sp...  1.08 us

profile of v3, /device:TPU:1, one launch (start us, length us, event | category | flops | bytes accessed | tf_op | source)
XLA Modules:
  0.0 31.5 jit_solution(1763179211277163457)
XLA Ops:
  0.6 29.8 %solve.1 = (f32[256,512]{1,0:T(8,128)S(1)}, f32[256,512]{1,0:T(8,128)S(1)}, f32[256,512]{1,0:T(8,128)S(1)}, f32[256,512]{1,0:T(8,128)S(1)}, f32[256,512]{1,0:T(8,128)S(1)}, /*index=5*/f32[8,128]{1,0:T(8,128)S(1)}) custom-call(f32[256,512]{1,0:T(8,128)} %refs_0_.1, f32[1,256]{1,0:T(1,128)} %bitcast.1, s32[1,256]{1,0:T(1,128)} %refs_2_.1, ...), custom_call_target="tpu_custom_call" | custom-call | tf_op jit(solution)/shard_map/solve/pallas_call | solution.py:713
  30.4 1.1 %combine.1 = (f32[256,512]{1,0:T(8,128)}, f32[256,512]{1,0:T(8,128)}) custom-call(f32[256,512]{1,0:T(8,128)S(1)} %get-tuple-element.8.z0, f32[256,512]{1,0:T(8,128)S(1)} %get-tuple-element.9.y, f32[256,512]{1,0:T(8,128)S(1)} %get-tuple-element.10.r0, f32[256,512]{1,0:T(8,128)S(1)} %get-tuple-element.11.q, f32[256,512]{1,0:T(8,128)S(1)} %get-tuple-element.12.w, ...), custom_call_target="tpu_custom_call" | custom-call | tf_op jit(solution)/shard_map/combine/pallas_call | solution.py:748

commit v4 on v3

--- a/solution.py
+++ b/solution.py
@@ -289,15 +289,28 @@
 
     barrier = pltpu.get_barrier_semaphore()
 
-    loads = [
-        pltpu.make_async_copy(source, target, in_sem.at[index])
-        for index, (source, target) in enumerate(zip(sources, inputs))
+    loads = {
+        index: pltpu.make_async_copy(sources[index], inputs[index], in_sem.at[index])
+        for index in range(1, len(inputs))
+    }
+    forcing_loads = [
+        pltpu.make_async_copy(
+            sources[0].at[:, pl.ds(at, width)],
+            forcing_ref.at[:, pl.ds(at, width)],
+            in_sem.at[len(inputs) + index],
+        )
+        for index, (at, width) in enumerate(((0, 128), (384, 128), (128, 256)))
     ]
-    for index in (2, 1, 0, *range(len(loads) - 1, 2, -1)):
-        loads[index].start()
+    loads[2].start()
+    forcing_loads[0].start()
+    forcing_loads[1].start()
+    loads[1].start()
     greeted = [by for by in range(-REACH, REACH + 1) if by != 0]
     for by in greeted:
         pl.semaphore_signal(barrier, inc=1, device_id=ring(by), device_id_type=MESH)
+    forcing_loads[2].start()
+    for index in range(len(inputs) - 1, 2, -1):
+        loads[index].start()
 
     stages = []
     while REACH << len(stages) < size // 2:
@@ -405,16 +418,14 @@
     kappa = sum(dot16(part, pick16, ((1,), (1,))) for part in split(kappa_rows, 3))[0:8]
     layer[1] = kappa[0:1]
     halo[REACH, 2:3] = kappa[0:1]
-    loads[0].wait()
     load_ref, r0_ref = field["load"], field["r0"]
 
     def permuted(matrix, value):
         return sum(dot16(matrix, part) for part in split(value, 3))
 
-    for index in (0, 3):
-        put(load_ref, index, permuted(pick16, tile(forcing_ref, index)))
-        put(r0_ref, index, shared_xy(tile(load_ref, index)))
-    first_face = face_of(r0_ref)
+    for copy in forcing_loads[:2]:
+        copy.wait()
+    first_face = shared_xy(permuted(pick16, face_of(forcing_ref)))
     pl.semaphore_wait(barrier, len(greeted))
     layer_copies = [
         remote(layer.at[1], layer.at[1 - by], layer_send.at[1 - by], layer_recv.at[1 - by], ring(by))
@@ -425,10 +436,10 @@
     edges = [send_faces(first_face, 0)]
     tell(0)
 
-    for index in (1, 2):
-        put(load_ref, index, permuted(pick16, tile(forcing_ref, index)))
-    for copy in loads[3:]:
-        copy.wait()
+    forcing_loads[2].wait()
+    load_ref[...] = permuted(pick16, forcing_ref[...])
+    for index in range(3, len(inputs)):
+        loads[index].wait()
     parts = split(load_ref[...], 2)
     first = table["gather"][32:48].astype(BF16)
     each = dot16(first, parts[0], ((1,), (1,)))
@@ -450,8 +461,8 @@
     upper_piece = stiff.astype(BF16)
     stiff_ref[0:NODES] = upper_piece
     stiff_ref[NODES:] = (stiff - upper_piece.astype(F32)).astype(BF16)
-    put(r0_ref, 1, shared_xy(tile(load_ref, 1)))
-    put(r0_ref, 2, shared_xy(tile(load_ref, 2)))
+    for index in range(4):
+        put(r0_ref, index, shared_xy(tile(load_ref, index)))
     gather = table["gather"][0:32].astype(BF16)
     gather_face = face_lanes(gather)
 
@@ -475,6 +486,8 @@
         stiff_face_ref[at + 64 : at + 128] = stiff_ref[piece + 448 : piece + 512]
     stiff_face_face = face_lanes(stiff_face_ref[...])
 
+    hear(0)
+    tell(1)
     for copy in layer_copies:
         copy.wait_recv()
     below9 = nine(jnp.broadcast_to(layer[0], (8, ROWS)))
@@ -500,19 +513,22 @@
     rough = coeff * (
         face_of(field["stiffened"]) + dot16(stacked, stiff_face_face)
     ) + mass_face * x_face
-    edges.append(send_faces(shared_xy(rough), 1))
     low, high = vertex_sums(kappa * rows0[0:8] + rows0[8:16])
     rest[NEAR, 0:1] = low
     rest[NEAR, 1:2] = high
     rest_copies = to_ring(rest, rest_send, rest_recv, NEAR)
     for copy in rest_copies.values():
         copy.start()
-
-    hear(0)
-    tell(1)
+    edges.append(send_faces(shared_xy(rough), 1))
+
+    hear(1)
+    tell(2)
     field["stiffened"][...] += dot16(stacked, stiff_face_ref[...])
     spread_table = table["spread"][...].astype(BF16)
     spread_face_table = table["spread_face"][...].astype(BF16)
+    spread_own_face = jnp.concatenate(
+        [face_lanes(spread_table[:, 0:NODES]), face_lanes(spread_table[:, NODES:])], 1
+    )
     for copy in halo_copies.values():
         copy.wait_recv()
     planes = list(range(-3, REACH + 1)) + list(range(1 - REACH, -3))
@@ -581,8 +597,6 @@
     face_image = face_of(field["qloc"])
     zero = jnp.zeros((ROWS, 128), F32)
     qy = inner(field["qloc"], field["x1"])
-    hear(1)
-    tell(2)
     back16 = pick.T.astype(BF16)
 
     def stored(value):
@@ -591,11 +605,11 @@
     sent_z0[...] = stored(field["z0"][...])
     sent_r0[...] = stored(r0_ref[...])
 
+    for copy in rest_copies.values():
+        copy.wait_recv()
     face = partial_face + faces_arrived(edges[1], 1)
     x_face, stacked, rows1 = outer(face, field["x1"], inner_rows)
     field["stiffened"][...] += dot16(stacked, stiff_face_ref[...])
-    for copy in rest_copies.values():
-        copy.wait_recv()
     target = jnp.concatenate([rest[NEAR + p, 0:1] for p in range(-3, 5)], 0) + jnp.concatenate(
         [rest[NEAR + p - 1, 1:2] for p in range(-3, 5)], 0
     )
@@ -609,6 +623,12 @@
     for _ in range(3):
         vert = start + swept(vert, level, from_above, from_below)
     (own,) = corners_of(vert, (3,))
+
+    own_pieces = columns(corner_pieces(own)).astype(BF16)
+    spread = dot16(own_pieces, spread_own_face)
+    y_face = x_face + spread[:, 0:128]
+    w_face = coeff * (face_of(field["stiffened"]) + spread[:, 128:256]) + mass_face * y_face
+    edges.append(send_faces(shared_xy(w_face), 2))
 
     def flipped(value, bit):
         corner = lax.broadcasted_iota(jnp.int32, value.shape, 0)
@@ -645,15 +665,12 @@
         remote(sums_ref.at[0], sums_ref.at[by], sum_send, sum_recv, ring(by)).start()
         return carry
 
-    lax.fori_loop(1, size, spread_sums, 0)
-
-    spread = dot16(columns(corner_pieces(own)).astype(BF16), spread_table)
-    applied(field["x1"], spread, field["y"], field["w"])
-    put(field["w"], 0, shared_xy(tile(field["w"], 0)))
-    put(field["w"], 3, shared_xy(tile(field["w"], 3)))
-    edges.append(send_faces(face_of(field["w"]), 2))
-    put(field["w"], 1, shared_xy(tile(field["w"], 1)))
-    put(field["w"], 2, shared_xy(tile(field["w"], 2)))
+    lax.fori_loop(size // 4, size, spread_sums, 0)
+    lax.fori_loop(1, size // 4, spread_sums, 0)
+
+    applied(field["x1"], dot16(own_pieces, spread_table), field["y"], field["w"])
+    for index in range(4):
+        put(field["w"], index, shared_xy(tile(field["w"], index)))
     put_face(field["q"], face)
     sent_y[...] = stored(field["y"][...])
     sent_q[...] = stored(field["q"][...])
@@ -727,7 +744,7 @@
             pltpu.VMEM((count, 3, ROWS), F32),
             pltpu.VMEM((close, 2, ROWS), F32),
             pltpu.VMEM((size, 1, 128), F32),
-            dma((len(operands),)),
+            dma((len(operands) + 3,)),
             dma((3,)),
             dma((3,)),
             dma((count,)),

time: 31.9 us -> 30.5 us (0.956)
  Pallas kernels: 30.9 us -> 29.8 us
    pallas_call x1, Pallas kernels: 29.8 us -> 28.7 us  [per_device(): pl.pallas_call(functools.partial(kernel, size), out_shape=(out,) * 5 + (s...]
where the time goes in v4:
time: 30.5 us; the launch traced here: 30.4 us
  Pallas kernels  29.8 us (98%)
  between operations  0.64 us (2%)
    pallas_call x1, Pallas kernels, per_device(): pl.pallas_call(functools.partial(kernel, size), out_shape=(out,) * 5 + (s...  28.7 us
    pallas_call x1, Pallas kernels, per_device(): pl.pallas_call(combine, out_shape=(out, out), in_specs=[vmem] * 6, out_sp...  1.08 us

profile of v4, /device:TPU:1, one launch (start us, length us, event | category | flops | bytes accessed | tf_op | source)
XLA Modules:
  0.0 30.4 jit_solution(4848291968211747886)
XLA Ops:
  0.6 28.7 %solve.1 = (f32[256,512]{1,0:T(8,128)S(1)}, f32[256,512]{1,0:T(8,128)S(1)}, f32[256,512]{1,0:T(8,128)S(1)}, f32[256,512]{1,0:T(8,128)S(1)}, f32[256,512]{1,0:T(8,128)S(1)}, /*index=5*/f32[8,128]{1,0:T(8,128)S(1)}) custom-call(f32[256,512]{1,0:T(8,128)} %refs_0_.1, f32[1,256]{1,0:T(1,128)} %bitcast.1, s32[1,256]{1,0:T(1,128)} %refs_2_.1, ...), custom_call_target="tpu_custom_call" | custom-call | tf_op jit(solution)/shard_map/solve/pallas_call | solution.py:730
  29.3 1.1 %combine.1 = (f32[256,512]{1,0:T(8,128)}, f32[256,512]{1,0:T(8,128)}) custom-call(f32[256,512]{1,0:T(8,128)S(1)} %get-tuple-element.8.z0, f32[256,512]{1,0:T(8,128)S(1)} %get-tuple-element.9.y, f32[256,512]{1,0:T(8,128)S(1)} %get-tuple-element.10.r0, f32[256,512]{1,0:T(8,128)S(1)} %get-tuple-element.11.q, f32[256,512]{1,0:T(8,128)S(1)} %get-tuple-element.12.w, ...), custom_call_target="tpu_custom_call" | custom-call | tf_op jit(solution)/shard_map/combine/pallas_call | solution.py:765

commit v5 on v4

--- a/solution.py
+++ b/solution.py
@@ -112,10 +112,13 @@
         fixed[mine] += REACT * mass[theirs]
     share, fixed = share.reshape(16, NODES), fixed.reshape(NODES)
     fixed_face = 2.0 * fixed[face]
-    share_face = np.zeros((48, 128))
-    share_face[0:16] = share[:, face]
-    share_face[16:32, :64] = share[:, facing[:64]]
-    share_face[32:48, 64:] = share[:, facing[64:]]
+    beside = np.zeros((24, 128))
+    beside[0:18:2, :64] = share[0:9, facing[:64]]
+    beside[1:18:2, 64:] = share[0:9, facing[64:]]
+    beside = pieces_of(beside, 2)
+    share_face = np.concatenate(
+        [share[:, face], beside[0], beside[1], beside[0], np.zeros((8, 128))], 0
+    )
 
     steep = full_stiff @ prolong
     heavy = REACT * mass_nodes[:, None] * prolong
@@ -276,12 +279,13 @@
     forcing_ref, kappa_ref, order_ref = inputs[:3]
     table = dict(zip(NAMES, inputs[3:]))
     field = dict(zip(FIELDS, take(len(FIELDS))))
-    coeff_ref, stiff_ref, stiff_face_ref = take(3)
+    coeff_ref, own_columns_ref, own_face_ref, inner_rows_ref, stiff_ref, stiff_face_ref = take(6)
     edge_out, edge_in, layer, halo, rest, sums_ref = take(6)
     in_sem, layer_send, layer_recv, halo_send, halo_recv = take(5)
     rest_send, rest_recv, edge_send, edge_recv, sum_send, sum_recv, known_sem = take(7)
 
-    me = lax.axis_index("elem") * 2 + lax.axis_index("face")
+    core = lax.axis_index("face")
+    me = lax.axis_index("elem") * 2 + core
 
     def ring(by):
         device = lax.rem(me + by + size, size)
@@ -361,7 +365,7 @@
         put(ref, 0, jnp.where(half, value, tile(ref, 0)))
         put(ref, 3, jnp.where(half, tile(ref, 3), value))
 
-    def send_faces(face, turn):
+    def send_faces(face, turn, both=True):
         top, bottom, part = face[0:128], face[128:256], half[0:128]
         edge_out[turn, 0] = jnp.where(part, pltpu.roll(top, 64, 1), bottom)
         edge_out[turn, 1] = jnp.where(part, top, pltpu.roll(bottom, 64, 1))
@@ -371,12 +375,13 @@
                 edge_in.at[turn, way],
                 edge_send.at[turn, way],
                 edge_recv.at[turn, way],
-                ring(by),
+                ring(1 - 2 * way),
             )
-            for way, by in ((0, 1), (1, -1))
+            for way in (1 - core, core)
         ]
-        for copy in copies:
-            copy.start()
+        copies[0].start()
+        if both:
+            copies[1].start()
         return copies
 
     def faces_arrived(copies, turn):
@@ -426,45 +431,11 @@
     for copy in forcing_loads[:2]:
         copy.wait()
     first_face = shared_xy(permuted(pick16, face_of(forcing_ref)))
-    pl.semaphore_wait(barrier, len(greeted))
-    layer_copies = [
-        remote(layer.at[1], layer.at[1 - by], layer_send.at[1 - by], layer_recv.at[1 - by], ring(by))
-        for by in (1, -1)
-    ]
-    for copy in layer_copies:
-        copy.start()
-    edges = [send_faces(first_face, 0)]
-    tell(0)
-
-    forcing_loads[2].wait()
-    load_ref[...] = permuted(pick16, forcing_ref[...])
-    for index in range(3, len(inputs)):
-        loads[index].wait()
-    parts = split(load_ref[...], 2)
-    first = table["gather"][32:48].astype(BF16)
-    each = dot16(first, parts[0], ((1,), (1,)))
-    each = each[0:8] + each[8:16] + dot16(first, parts[1], ((1,), (1,)))[0:8]
-    low, high = vertex_sums(each)
-    halo[REACH, 0:1] = low
-    halo[REACH, 1:2] = high
-    halo_copies = to_ring(halo, halo_send, halo_recv, REACH)
-    for copy in halo_copies.values():
-        copy.start()
     own9 = nine(kappa)
     own_rows = [plane[0:1] for plane in own9] + [jnp.zeros((7, ROWS), F32)]
     own_columns = columns(own_rows)
     coeff_ref[...] = jnp.broadcast_to(own_columns[:, 4:5], (ROWS, 128))
-    fixed, mass = table["rows"][0:1], table["rows"][1:2]
-    fixed_face, mass_face = table["rows"][2:3, 0:128], table["rows"][3:4, 0:128]
-    field["inverse"][...] = 1.0 / (dot(own_columns, table["share"][...]) + fixed)
-    stiff = table["stiff"][...]
-    upper_piece = stiff.astype(BF16)
-    stiff_ref[0:NODES] = upper_piece
-    stiff_ref[NODES:] = (stiff - upper_piece.astype(F32)).astype(BF16)
-    for index in range(4):
-        put(r0_ref, index, shared_xy(tile(load_ref, index)))
-    gather = table["gather"][0:32].astype(BF16)
-    gather_face = face_lanes(gather)
+    own_columns_ref[...] = own_columns
 
     def interior(value, x_ref):
         inverse = field["inverse"]
@@ -478,26 +449,84 @@
         field["stiffened"][...] = (
             dot16(parts[0], high) + dot16(parts[1], high) + dot16(parts[0], low)
         )
-        return gathered(gather, parts)
-
-    inner_rows = interior(r0_ref, field["x0"])
-    for at, piece in ((0, 0), (128, 0), (256, NODES)):
-        stiff_face_ref[at : at + 64] = stiff_ref[piece : piece + 64]
-        stiff_face_ref[at + 64 : at + 128] = stiff_ref[piece + 448 : piece + 512]
+        return gathered(table["gather"][0:32].astype(BF16), parts)
+
+    def prepare_halo():
+        forcing_loads[2].wait()
+        load_ref[...] = permuted(pick16, forcing_ref[...])
+        for index in range(3, len(inputs)):
+            loads[index].wait()
+        parts = split(load_ref[...], 2)
+        first = table["gather"][32:48].astype(BF16)
+        each = dot16(first, parts[0], ((1,), (1,)))
+        each = each[0:8] + each[8:16] + dot16(first, parts[1], ((1,), (1,)))[0:8]
+        low, high = vertex_sums(each)
+        halo[REACH, 0:1] = low
+        halo[REACH, 1:2] = high
+
+    def prepare_interior():
+        own_columns = own_columns_ref[...]
+        fixed = table["rows"][0:1]
+        field["inverse"][...] = 1.0 / (dot(own_columns, table["share"][...]) + fixed)
+        own_face_ref[...] = dot(own_columns, table["share_face"][0:16]) + table["rows"][2:3, 0:128]
+        stiff = table["stiff"][...]
+        upper_piece = stiff.astype(BF16)
+        stiff_ref[0:NODES] = upper_piece
+        stiff_ref[NODES:] = (stiff - upper_piece.astype(F32)).astype(BF16)
+        for index in range(4):
+            put(r0_ref, index, shared_xy(tile(load_ref, index)))
+        inner_rows_ref[...] = interior(r0_ref, field["x0"])
+        for at, piece in ((0, 0), (128, 0), (256, NODES)):
+            stiff_face_ref[at : at + 64] = stiff_ref[piece : piece + 64]
+            stiff_face_ref[at + 64 : at + 128] = stiff_ref[piece + 448 : piece + 512]
+
+    ahead = me < REACH
+
+    @pl.when(ahead)
+    def _():
+        prepare_halo()
+        prepare_interior()
+
+    pl.semaphore_wait(barrier, len(greeted))
+    layer_copies = [
+        remote(layer.at[1], layer.at[1 - by], layer_send.at[1 - by], layer_recv.at[1 - by], ring(by))
+        for by in (1, -1)
+    ]
+    for copy in layer_copies:
+        copy.start()
+    edges = [send_faces(first_face, 0)]
+    tell(0)
+
+    @pl.when(jnp.logical_not(ahead))
+    def _():
+        prepare_halo()
+
+    halo_copies = to_ring(halo, halo_send, halo_recv, REACH)
+    for copy in halo_copies.values():
+        copy.start()
+
+    @pl.when(jnp.logical_not(ahead))
+    def _():
+        prepare_interior()
+
+    inner_rows = inner_rows_ref[...]
+    mass, mass_face = table["rows"][1:2], table["rows"][3:4, 0:128]
+    own_face = own_face_ref[...]
+    share_two = table["share_face"][16:96].astype(BF16)
+    gather = table["gather"][0:32].astype(BF16)
+    gather_face = face_lanes(gather)
     stiff_face_face = face_lanes(stiff_face_ref[...])
 
     hear(0)
     tell(1)
     for copy in layer_copies:
         copy.wait_recv()
-    below9 = nine(jnp.broadcast_to(layer[0], (8, ROWS)))
-    above9 = nine(jnp.broadcast_to(layer[2], (8, ROWS)))
-    pad = [jnp.zeros((7, ROWS), F32)]
-    three = columns(
-        own_rows + [p[0:1] for p in below9] + pad + [p[0:1] for p in above9] + pad
-    )
-    inverse_face = 1.0 / (dot(three, table["share_face"][...]) + fixed_face)
-    coeff_beside = jnp.where(half, three[:, 20:21], three[:, 36:37])
+    two = jnp.concatenate([layer[0], layer[2], jnp.zeros((6, ROWS), F32)], 0)
+    two9 = jnp.concatenate([plane[0:2] for plane in nine(two)] + [two[2:8]], 0)
+    two_pieces = [part.astype(F32) for part in split(two9, 2)]
+    two_columns = columns([two_pieces[0], two_pieces[0], two_pieces[1], two])
+    inverse_face = 1.0 / (own_face + dot16(two_columns.astype(BF16), share_two))
+    coeff_beside = jnp.where(half, two_columns[:, 72:73], two_columns[:, 73:74])
     coeff = coeff_ref[...]
     face = first_face + faces_arrived(edges[0], 0)
     put_face(r0_ref, face)
@@ -507,12 +536,11 @@
         put_face(x_ref, x_face)
         parts = split(x_face, 2)
         rows = rows + gathered(gather_face, parts)
-        return x_face, jnp.concatenate([parts[0], parts[1], parts[0]], 1), rows
-
-    x_face, stacked, rows0 = outer(face, field["x0"], inner_rows)
-    rough = coeff * (
-        face_of(field["stiffened"]) + dot16(stacked, stiff_face_face)
-    ) + mass_face * x_face
+        stacked = jnp.concatenate([parts[0], parts[1], parts[0]], 1)
+        return x_face, stacked, rows, dot16(stacked, stiff_face_face)
+
+    x_face, stacked, rows0, steep_face = outer(face, field["x0"], inner_rows)
+    rough = coeff * (face_of(field["stiffened"]) + steep_face) + mass_face * x_face
     low, high = vertex_sums(kappa * rows0[0:8] + rows0[8:16])
     rest[NEAR, 0:1] = low
     rest[NEAR, 1:2] = high
@@ -595,6 +623,17 @@
     inner_rows = interior(field["q"], field["x1"])
 
     face_image = face_of(field["qloc"])
+    steep_inner = face_of(field["stiffened"])
+    yw = total(
+        sum(
+            tile(field["x1"], index)
+            * (
+                coeff * tile(field["stiffened"], index)
+                + mass[:, 128 * index : 128 * index + 128] * tile(field["x1"], index)
+            )
+            for index in range(4)
+        )
+    )
     zero = jnp.zeros((ROWS, 128), F32)
     qy = inner(field["qloc"], field["x1"])
     back16 = pick.T.astype(BF16)
@@ -608,8 +647,7 @@
     for copy in rest_copies.values():
         copy.wait_recv()
     face = partial_face + faces_arrived(edges[1], 1)
-    x_face, stacked, rows1 = outer(face, field["x1"], inner_rows)
-    field["stiffened"][...] += dot16(stacked, stiff_face_ref[...])
+    x_face, stacked, rows1, steep_face = outer(face, field["x1"], inner_rows)
     target = jnp.concatenate([rest[NEAR + p, 0:1] for p in range(-3, 5)], 0) + jnp.concatenate(
         [rest[NEAR + p - 1, 1:2] for p in range(-3, 5)], 0
     )
@@ -627,8 +665,8 @@
     own_pieces = columns(corner_pieces(own)).astype(BF16)
     spread = dot16(own_pieces, spread_own_face)
     y_face = x_face + spread[:, 0:128]
-    w_face = coeff * (face_of(field["stiffened"]) + spread[:, 128:256]) + mass_face * y_face
-    edges.append(send_faces(shared_xy(w_face), 2))
+    w_face = coeff * (steep_inner + steep_face + spread[:, 128:256]) + mass_face * y_face
+    late_face = shared_xy(w_face)
 
     def flipped(value, bit):
         corner = lax.broadcasted_iota(jnp.int32, value.shape, 0)
@@ -646,13 +684,10 @@
         kappa * (steep + 2.0 * rows1[0:8]) + (REACT * weighed + 2.0 * rows1[8:16])
     )
     qy = qy + total(face_image * x_face) + jnp.sum((start * vert / -damp[0:8])[3:4], keepdims=True)
-    yw = jnp.sum(energy, keepdims=True)
-    image = [
-        coeff * tile(field["stiffened"], index)
-        + mass[:, 128 * index : 128 * index + 128] * tile(field["x1"], index)
-        for index in range(4)
-    ]
-    yw = yw + total(sum(image[index] * tile(field["x1"], index) for index in range(4)))
+    yw = yw + jnp.sum(energy, keepdims=True)
+    yw = yw + total(
+        x_face * (coeff * (2.0 * steep_inner + steep_face) + mass_face * x_face)
+    )
 
     hear(2)
     lane = lanes((1, 128))
@@ -661,13 +696,20 @@
         mine = jnp.where(lane == index, value, mine)
     sums_ref[0] = mine
 
-    def spread_sums(by, carry):
+    def send_sums(by):
         remote(sums_ref.at[0], sums_ref.at[by], sum_send, sum_recv, ring(by)).start()
+
+    def both_ways(by, carry):
+        send_sums(by)
+        send_sums(size - by)
         return carry
 
-    lax.fori_loop(size // 4, size, spread_sums, 0)
-    lax.fori_loop(1, size // 4, spread_sums, 0)
-
+    lax.fori_loop(1, REACH, both_ways, 0)
+    edges.append(send_faces(late_face, 2))
+    lax.fori_loop(REACH, size // 2, both_ways, 0)
+    send_sums(size // 2)
+
+    field["stiffened"][...] += dot16(stacked, stiff_face_ref[...])
     applied(field["x1"], dot16(own_pieces, spread_table), field["y"], field["w"])
     for index in range(4):
         put(field["w"], index, shared_xy(tile(field["w"], index)))
@@ -736,6 +778,9 @@
         + [pltpu.VMEM((ROWS, NODES), F32)] * len(FIELDS)
         + [
             pltpu.VMEM((ROWS, 128), F32),
+            pltpu.VMEM((ROWS, 16), F32),
+            pltpu.VMEM((ROWS, 128), F32),
+            pltpu.VMEM((16, ROWS), F32),
             pltpu.VMEM((2 * NODES, NODES), BF16),
             pltpu.VMEM((384, NODES), BF16),
             pltpu.VMEM((3, 2, 128, 128), F32),

time: 30.5 us -> 29.5 us (0.967)
  Pallas kernels: 29.8 us -> 28.5 us
    pallas_call x1, Pallas kernels: 28.7 us -> 27.5 us  [per_device(): pl.pallas_call(functools.partial(kernel, size), out_shape=(out,) * 5 + (s...]
where the time goes in v5:
time: 29.5 us; the launch traced here: 29.2 us
  Pallas kernels  28.5 us (97%)
  between operations  0.64 us (2%)
    pallas_call x1, Pallas kernels, per_device(): pl.pallas_call(functools.partial(kernel, size), out_shape=(out,) * 5 + (s...  27.5 us
    pallas_call x1, Pallas kernels, per_device(): pl.pallas_call(combine, out_shape=(out, out), in_specs=[vmem] * 6, out_sp...  1.08 us

profile of v5, /device:TPU:1, one launch (start us, length us, event | category | flops | bytes accessed | tf_op | source)
XLA Modules:
  0.0 29.2 jit_solution(13859602152329426224)
XLA Ops:
  0.6 27.5 %solve.1 = (f32[256,512]{1,0:T(8,128)S(1)}, f32[256,512]{1,0:T(8,128)S(1)}, f32[256,512]{1,0:T(8,128)S(1)}, f32[256,512]{1,0:T(8,128)S(1)}, f32[256,512]{1,0:T(8,128)S(1)}, /*index=5*/f32[8,128]{1,0:T(8,128)S(1)}) custom-call(f32[256,512]{1,0:T(8,128)} %refs_0_.1, f32[1,256]{1,0:T(1,128)} %bitcast.1, s32[1,256]{1,0:T(1,128)} %refs_2_.1, ...), custom_call_target="tpu_custom_call" | custom-call | tf_op jit(solution)/shard_map/solve/pallas_call | solution.py:772
  28.1 1.1 %combine.1 = (f32[256,512]{1,0:T(8,128)}, f32[256,512]{1,0:T(8,128)}) custom-call(f32[256,512]{1,0:T(8,128)S(1)} %get-tuple-element.8.z0, f32[256,512]{1,0:T(8,128)S(1)} %get-tuple-element.9.y, f32[256,512]{1,0:T(8,128)S(1)} %get-tuple-element.10.r0, f32[256,512]{1,0:T(8,128)S(1)} %get-tuple-element.11.q, f32[256,512]{1,0:T(8,128)S(1)} %get-tuple-element.12.w, ...), custom_call_target="tpu_custom_call" | custom-call | tf_op jit(solution)/shard_map/combine/pallas_call | solution.py:810

commit v6 on v5

--- a/solution.py
+++ b/solution.py
@@ -177,16 +177,22 @@
     return lax.broadcasted_iota(jnp.int32, shape, len(shape) - 1)
 
 
-def roll_x(plane, by):
+def shifted(plane, dy, dx):
     size = plane.shape[1]
-    along = lanes(plane.shape) % EX
-    inside = pltpu.roll(plane, by % size, 1)
-    around = pltpu.roll(plane, (by - EX * by) % size, 1)
-    return jnp.where(along == (0 if by == 1 else EX - 1), around, inside)
-
-
-def roll_y(plane, by):
-    return pltpu.roll(plane, (by * EX) % plane.shape[1], 1)
+    if dy == 0 and dx == 0:
+        return plane
+    inside = pltpu.roll(plane, -(EX * dy + dx) % size, 1)
+    if dx == 0:
+        return inside
+    around = pltpu.roll(plane, -(EX * dy + dx - EX * dx) % size, 1)
+    return jnp.where(lanes(plane.shape) % EX == (EX - 1 if dx == 1 else 0), around, inside)
+
+
+def added(terms):
+    terms = list(terms)
+    while len(terms) > 1:
+        terms = [sum(terms[at : at + 2]) for at in range(0, len(terms), 2)]
+    return terms[0]
 
 
 def down(plane):
@@ -211,15 +217,11 @@
 
 
 def four(layer):
-    moved = [layer, roll_x(layer, 1)]
-    return moved + [roll_y(moved[0], 1), roll_y(moved[1], 1)]
+    return [shifted(layer, 0, 0), shifted(layer, 0, -1), shifted(layer, -1, 0), shifted(layer, -1, -1)]
 
 
 def nine(layer):
-    side = {0: layer, 1: roll_x(layer, -1), -1: roll_x(layer, 1)}
-    return [
-        side[dx] if dy == 0 else roll_y(side[dx], -dy) for dy in (-1, 0, 1) for dx in (-1, 0, 1)
-    ]
+    return [shifted(layer, dy, dx) for dy in (-1, 0, 1) for dx in (-1, 0, 1)]
 
 
 def coarse_stencil(layer4, planes):
@@ -240,17 +242,11 @@
 
 
 def swept(vert, level, from_above, from_below):
-    along = {0: vert, 1: roll_x(vert, -1), -1: roll_x(vert, 1)}
-    spread = {}
-    for dx, value in along.items():
-        spread[0, dx] = value
-        spread[1, dx] = roll_y(value, -1)
-        spread[-1, dx] = roll_y(value, 1)
-    total = (1.0 - OMEGA) * vert
-    total += sum(level[key] * spread[key] for key in level)
-    total += down(sum(from_above[key] * spread[key] for key in from_above))
-    total += up(sum(from_below[key] * spread[key] for key in from_below))
-    return total
+    spread = {key: shifted(vert, *key) for key in from_above}
+    above = down(added(from_above[key] * spread[key] for key in from_above))
+    below = up(added(from_below[key] * spread[key] for key in from_below))
+    here = added([(1.0 - OMEGA) * vert] + [level[key] * spread[key] for key in level])
+    return here + (above + below)
 
 
 NAMES = (
@@ -292,6 +288,9 @@
         return lax.div(device, 2), lax.rem(device, 2)
 
     barrier = pltpu.get_barrier_semaphore()
+    greeted = [by for by in range(-REACH, REACH + 1) if by != 0]
+    for by in greeted:
+        pl.semaphore_signal(barrier, inc=1, device_id=ring(by), device_id_type=MESH)
 
     loads = {
         index: pltpu.make_async_copy(sources[index], inputs[index], in_sem.at[index])
@@ -309,9 +308,6 @@
     forcing_loads[0].start()
     forcing_loads[1].start()
     loads[1].start()
-    greeted = [by for by in range(-REACH, REACH + 1) if by != 0]
-    for by in greeted:
-        pl.semaphore_signal(barrier, inc=1, device_id=ring(by), device_id_type=MESH)
     forcing_loads[2].start()
     for index in range(len(inputs) - 1, 2, -1):
         loads[index].start()
@@ -394,8 +390,9 @@
 
     def vertex_sums(each):
         corner = lax.broadcasted_iota(jnp.int32, each.shape, 0)
-        each = jnp.where(corner % 2 == 1, roll_x(each, 1), each)
-        each = jnp.where(corner // 2 % 2 == 1, roll_y(each, 1), each)
+        even = jnp.where(corner // 2 % 2 == 1, shifted(each, -1, 0), each)
+        odd = jnp.where(corner // 2 % 2 == 1, shifted(each, -1, -1), shifted(each, 0, -1))
+        each = jnp.where(corner % 2 == 1, odd, even)
         low = jnp.sum(each[0:4], axis=0, keepdims=True)
         high = jnp.sum(each[4:8], axis=0, keepdims=True)
         return low, high
@@ -579,8 +576,7 @@
     remainder = (vert - swept(vert, level, from_above, from_below))[0:8]
 
     def corners_of(vert, lower):
-        one = roll_x(vert, -1)
-        found = [vert, one, roll_y(vert, -1), roll_y(one, -1)]
+        found = [shifted(vert, *key) for key in ((0, 0), (0, 1), (1, 0), (1, 1))]
         return [
             jnp.concatenate(
                 [c[k : k + 1] for c in found] + [c[k + 1 : k + 2] for c in found], 0
@@ -597,7 +593,11 @@
     beside = shared_xy(coeff_beside * beside[:, 0:128] + beside[:, 128:256])
 
     def total(value):
-        return jnp.sum(jnp.sum(value.reshape(ROWS // 8, 8, 128), axis=0), axis=(0, 1), keepdims=True)
+        quarter = ROWS // 4
+        value = added(value[at * quarter : at * quarter + quarter] for at in range(4))
+        return jnp.sum(
+            jnp.sum(value.reshape(quarter // 8, 8, 128), axis=0), axis=(0, 1), keepdims=True
+        )
 
     def applied(x_ref, spread, z_ref, image_ref):
         for index in range(4):
@@ -612,7 +612,7 @@
             )
 
     def inner(left, right):
-        return total(sum(tile(left, index) * tile(right, index) for index in range(4)))
+        return total(added(tile(left, index) * tile(right, index) for index in range(4)))
 
     applied(field["x0"], spread, field["z0"], field["qloc"])
     rz = inner(load_ref, field["z0"])
@@ -696,18 +696,14 @@
         mine = jnp.where(lane == index, value, mine)
     sums_ref[0] = mine
 
-    def send_sums(by):
+    def send_sums(turn, carry):
+        by = lax.rem(turn + jnp.where(turn >= me, 1, 0) - me + size, size)
         remote(sums_ref.at[0], sums_ref.at[by], sum_send, sum_recv, ring(by)).start()
-
-    def both_ways(by, carry):
-        send_sums(by)
-        send_sums(size - by)
         return carry
 
-    lax.fori_loop(1, REACH, both_ways, 0)
+    lax.fori_loop(0, REACH, send_sums, 0)
     edges.append(send_faces(late_face, 2))
-    lax.fori_loop(REACH, size // 2, both_ways, 0)
-    send_sums(size // 2)
+    lax.fori_loop(REACH, size - 1, send_sums, 0)
 
     field["stiffened"][...] += dot16(stacked, stiff_face_ref[...])
     applied(field["x1"], dot16(own_pieces, spread_table), field["y"], field["w"])
@@ -723,7 +719,9 @@
     others = sums_ref.at[pl.ds(1, size - 1)]
     all_sums = remote(others, others, sum_send, sum_recv, ring(1))
     all_sums.wait_recv()
-    sums = jnp.sum(sums_ref[...], axis=0)
+    eighth = size // 8
+    sums = added(sums_ref[at * eighth : at * eighth + eighth] for at in range(8))
+    sums = jnp.sum(sums, axis=0)
     rz, zq, qy, yw = (sums[:, index : index + 1] for index in range(4))
     first = rz / zq
     gamma = first * first * qy - rz

time: 29.5 us -> 29 us (0.983)
  Pallas kernels: 28.5 us -> 28.2 us
    pallas_call x1, Pallas kernels: 27.5 us -> 27.2 us  [per_device(): pl.pallas_call(functools.partial(kernel, size), out_shape=(out,) * 5 + (s...]
where the time goes in v6:
time: 29 us; the launch traced here: 28.9 us
  Pallas kernels  28.2 us (97%)
  between operations  0.64 us (2%)
    pallas_call x1, Pallas kernels, per_device(): pl.pallas_call(functools.partial(kernel, size), out_shape=(out,) * 5 + (s...  27.2 us
    pallas_call x1, Pallas kernels, per_device(): pl.pallas_call(combine, out_shape=(out, out), in_specs=[vmem] * 6, out_sp...  1.08 us

profile of v6, /device:TPU:1, one launch (start us, length us, event | category | flops | bytes accessed | tf_op | source)
XLA Modules:
  0.0 28.9 jit_solution(10647104769232626858)
XLA Ops:
  0.6 27.2 %solve.1 = (f32[256,512]{1,0:T(8,128)S(1)}, f32[256,512]{1,0:T(8,128)S(1)}, f32[256,512]{1,0:T(8,128)S(1)}, f32[256,512]{1,0:T(8,128)S(1)}, f32[256,512]{1,0:T(8,128)S(1)}, /*index=5*/f32[8,128]{1,0:T(8,128)S(1)}) custom-call(f32[256,512]{1,0:T(8,128)} %refs_0_.1, f32[1,256]{1,0:T(1,128)} %bitcast.1, s32[1,256]{1,0:T(1,128)} %refs_2_.1, ...), custom_call_target="tpu_custom_call" | custom-call | tf_op jit(solution)/shard_map/solve/pallas_call | solution.py:770
  27.8 1.1 %combine.1 = (f32[256,512]{1,0:T(8,128)}, f32[256,512]{1,0:T(8,128)}) custom-call(f32[256,512]{1,0:T(8,128)S(1)} %get-tuple-element.8.z0, f32[256,512]{1,0:T(8,128)S(1)} %get-tuple-element.9.y, f32[256,512]{1,0:T(8,128)S(1)} %get-tuple-element.10.r0, f32[256,512]{1,0:T(8,128)S(1)} %get-tuple-element.11.q, f32[256,512]{1,0:T(8,128)S(1)} %get-tuple-element.12.w, ...), custom_call_target="tpu_custom_call" | custom-call | tf_op jit(solution)/shard_map/combine/pallas_call | solution.py:808

commit v7 on v6

--- a/solution.py
+++ b/solution.py
@@ -338,13 +338,17 @@
             device_id_type=MESH,
         )
 
+    def slot(place, reach):
+        return 2 * reach if place == reach else place - (place > reach)
+
     def to_ring(buffer, send, recv, reach):
-        found = {}
         for by in sorted(range(-reach, reach + 1), key=abs):
             if by != 0:
-                at = reach - by
-                found[by] = remote(buffer.at[reach], buffer.at[at], send.at[at], recv.at[at], ring(by))
-        return found
+                remote(
+                    buffer.at[2 * reach], buffer.at[slot(reach - by, reach)], send, recv, ring(by)
+                ).start()
+        others = buffer.at[pl.ds(0, 2 * reach)]
+        return remote(others, others, send, recv, ring(1))
 
     half = lanes((ROWS, 128)) < 64
 
@@ -361,7 +365,7 @@
         put(ref, 0, jnp.where(half, value, tile(ref, 0)))
         put(ref, 3, jnp.where(half, tile(ref, 3), value))
 
-    def send_faces(face, turn, both=True):
+    def send_faces(face, turn):
         top, bottom, part = face[0:128], face[128:256], half[0:128]
         edge_out[turn, 0] = jnp.where(part, pltpu.roll(top, 64, 1), bottom)
         edge_out[turn, 1] = jnp.where(part, top, pltpu.roll(bottom, 64, 1))
@@ -369,20 +373,20 @@
             remote(
                 edge_out.at[turn, way],
                 edge_in.at[turn, way],
-                edge_send.at[turn, way],
-                edge_recv.at[turn, way],
+                edge_send.at[turn],
+                edge_recv.at[turn],
                 ring(1 - 2 * way),
             )
             for way in (1 - core, core)
         ]
-        copies[0].start()
-        if both:
-            copies[1].start()
-        return copies
+        for copy in copies:
+            copy.start()
+        return remote(
+            edge_out.at[turn], edge_in.at[turn], edge_send.at[turn], edge_recv.at[turn], ring(1)
+        )
 
     def faces_arrived(copies, turn):
-        for copy in copies:
-            copy.wait_recv()
+        copies.wait_recv()
         below, above, part = edge_in[turn, 0], edge_in[turn, 1], half[0:128]
         top = jnp.where(part, below, pltpu.roll(above, 64, 1))
         bottom = jnp.where(part, pltpu.roll(below, 64, 1), above)
@@ -418,8 +422,8 @@
     loads[1].wait()
     kappa_rows = jnp.broadcast_to(kappa_ref[...], (16, ROWS))
     kappa = sum(dot16(part, pick16, ((1,), (1,))) for part in split(kappa_rows, 3))[0:8]
-    layer[1] = kappa[0:1]
-    halo[REACH, 2:3] = kappa[0:1]
+    layer[2] = kappa[0:1]
+    halo[2 * REACH, 2:3] = kappa[0:1]
     load_ref, r0_ref = field["load"], field["r0"]
 
     def permuted(matrix, value):
@@ -458,8 +462,8 @@
         each = dot16(first, parts[0], ((1,), (1,)))
         each = each[0:8] + each[8:16] + dot16(first, parts[1], ((1,), (1,)))[0:8]
         low, high = vertex_sums(each)
-        halo[REACH, 0:1] = low
-        halo[REACH, 1:2] = high
+        halo[2 * REACH, 0:1] = low
+        halo[2 * REACH, 1:2] = high
 
     def prepare_interior():
         own_columns = own_columns_ref[...]
@@ -485,12 +489,7 @@
         prepare_interior()
 
     pl.semaphore_wait(barrier, len(greeted))
-    layer_copies = [
-        remote(layer.at[1], layer.at[1 - by], layer_send.at[1 - by], layer_recv.at[1 - by], ring(by))
-        for by in (1, -1)
-    ]
-    for copy in layer_copies:
-        copy.start()
+    layer_copies = to_ring(layer, layer_send, layer_recv, 1)
     edges = [send_faces(first_face, 0)]
     tell(0)
 
@@ -499,8 +498,6 @@
         prepare_halo()
 
     halo_copies = to_ring(halo, halo_send, halo_recv, REACH)
-    for copy in halo_copies.values():
-        copy.start()
 
     @pl.when(jnp.logical_not(ahead))
     def _():
@@ -516,9 +513,8 @@
 
     hear(0)
     tell(1)
-    for copy in layer_copies:
-        copy.wait_recv()
-    two = jnp.concatenate([layer[0], layer[2], jnp.zeros((6, ROWS), F32)], 0)
+    layer_copies.wait_recv()
+    two = jnp.concatenate([layer[0], layer[1], jnp.zeros((6, ROWS), F32)], 0)
     two9 = jnp.concatenate([plane[0:2] for plane in nine(two)] + [two[2:8]], 0)
     two_pieces = [part.astype(F32) for part in split(two9, 2)]
     two_columns = columns([two_pieces[0], two_pieces[0], two_pieces[1], two])
@@ -539,11 +535,9 @@
     x_face, stacked, rows0, steep_face = outer(face, field["x0"], inner_rows)
     rough = coeff * (face_of(field["stiffened"]) + steep_face) + mass_face * x_face
     low, high = vertex_sums(kappa * rows0[0:8] + rows0[8:16])
-    rest[NEAR, 0:1] = low
-    rest[NEAR, 1:2] = high
+    rest[2 * NEAR, 0:1] = low
+    rest[2 * NEAR, 1:2] = high
     rest_copies = to_ring(rest, rest_send, rest_recv, NEAR)
-    for copy in rest_copies.values():
-        copy.start()
     edges.append(send_faces(shared_xy(rough), 1))
 
     hear(1)
@@ -554,12 +548,12 @@
     spread_own_face = jnp.concatenate(
         [face_lanes(spread_table[:, 0:NODES]), face_lanes(spread_table[:, NODES:])], 1
     )
-    for copy in halo_copies.values():
-        copy.wait_recv()
+    halo_copies.wait_recv()
     planes = list(range(-3, REACH + 1)) + list(range(1 - REACH, -3))
 
     def halo_rows(shift, which):
-        return jnp.concatenate([halo[REACH + p + shift, which : which + 1] for p in planes], 0)
+        places = [slot(REACH + p + shift, REACH) for p in planes]
+        return jnp.concatenate([halo[place, which : which + 1] for place in places], 0)
 
     under4, over4 = four(halo_rows(-1, 2)), four(halo_rows(0, 2))
     both4 = [a + b for a, b in zip(under4, over4)]
@@ -644,13 +638,12 @@
     sent_z0[...] = stored(field["z0"][...])
     sent_r0[...] = stored(r0_ref[...])
 
-    for copy in rest_copies.values():
-        copy.wait_recv()
+    rest_copies.wait_recv()
     face = partial_face + faces_arrived(edges[1], 1)
     x_face, stacked, rows1, steep_face = outer(face, field["x1"], inner_rows)
-    target = jnp.concatenate([rest[NEAR + p, 0:1] for p in range(-3, 5)], 0) + jnp.concatenate(
-        [rest[NEAR + p - 1, 1:2] for p in range(-3, 5)], 0
-    )
+    target = jnp.concatenate(
+        [rest[slot(NEAR + p, NEAR), 0:1] for p in range(-3, 5)], 0
+    ) + jnp.concatenate([rest[slot(NEAR + p - 1, NEAR), 1:2] for p in range(-3, 5)], 0)
 
     def top(parts):
         return {key: value[0:8] for key, value in parts.items()}
@@ -713,11 +706,14 @@
     sent_y[...] = stored(field["y"][...])
     sent_q[...] = stored(field["q"][...])
     sent_w[...] = stored(field["w"][...])
+    others = sums_ref.at[pl.ds(1, size - 1)]
+    all_sums = remote(others, others, sum_send, sum_recv, ring(1))
+    all_sums.wait_send()
+    for copies in [layer_copies, halo_copies, rest_copies] + edges:
+        copies.wait_send()
     face = stored(faces_arrived(edges[2], 2))
     sent_w[:, 0:128] += jnp.where(half, face, zero)
     sent_w[:, 384:512] += jnp.where(half, zero, face)
-    others = sums_ref.at[pl.ds(1, size - 1)]
-    all_sums = remote(others, others, sum_send, sum_recv, ring(1))
     all_sums.wait_recv()
     eighth = size // 8
     sums = added(sums_ref[at * eighth : at * eighth + eighth] for at in range(8))
@@ -730,11 +726,6 @@
     straight, bent = first + second * grown, first * second
     steps_ref[0:1] = jnp.broadcast_to(straight, (1, 128))
     steps_ref[1:2] = jnp.broadcast_to(bent, (1, 128))
-
-    all_sums.wait_send()
-    for copies in [layer_copies, halo_copies.values(), rest_copies.values()] + edges:
-        for copy in copies:
-            copy.wait_send()
 
 
 def combine(z0, y, r0, q, w, steps, solution_ref, residual_ref, solution_part, residual_part, sem):
@@ -788,14 +779,14 @@
             pltpu.VMEM((close, 2, ROWS), F32),
             pltpu.VMEM((size, 1, 128), F32),
             dma((len(operands) + 3,)),
+            dma,
+            dma,
+            dma,
+            dma,
+            dma,
+            dma,
             dma((3,)),
             dma((3,)),
-            dma((count,)),
-            dma((count,)),
-            dma((close,)),
-            dma((close,)),
-            dma((3, 2)),
-            dma((3, 2)),
             dma,
             dma,
             pltpu.SemaphoreType.REGULAR((3, 2)),

time: 29 us -> 28.4 us (0.979)
  Pallas kernels: 28.2 us -> 27.7 us
    pallas_call x1, Pallas kernels: 27.2 us -> 26.6 us  [per_device(): pl.pallas_call(functools.partial(kernel, size), out_shape=(out,) * 5 + (s...]
where the time goes in v7:
time: 28.4 us; the launch traced here: 28.3 us
  Pallas kernels  27.7 us (98%)
  between operations  0.64 us (2%)
    pallas_call x1, Pallas kernels, per_device(): pl.pallas_call(functools.partial(kernel, size), out_shape=(out,) * 5 + (s...  26.6 us
    pallas_call x1, Pallas kernels, per_device(): pl.pallas_call(combine, out_shape=(out, out), in_specs=[vmem] * 6, out_sp...  1.08 us

profile of v7, /device:TPU:1, one launch (start us, length us, event | category | flops | bytes accessed | tf_op | source)
XLA Modules:
  0.0 28.3 jit_solution(11726874603012739260)
XLA Ops:
  0.6 26.6 %solve.1 = (f32[256,512]{1,0:T(8,128)S(1)}, f32[256,512]{1,0:T(8,128)S(1)}, f32[256,512]{1,0:T(8,128)S(1)}, f32[256,512]{1,0:T(8,128)S(1)}, f32[256,512]{1,0:T(8,128)S(1)}, /*index=5*/f32[8,128]{1,0:T(8,128)S(1)}) custom-call(f32[256,512]{1,0:T(8,128)} %refs_0_.1, f32[1,256]{1,0:T(1,128)} %bitcast.1, s32[1,256]{1,0:T(1,128)} %refs_2_.1, ...), custom_call_target="tpu_custom_call" | custom-call | tf_op jit(solution)/shard_map/solve/pallas_call | solution.py:761
  27.2 1.1 %combine.1 = (f32[256,512]{1,0:T(8,128)}, f32[256,512]{1,0:T(8,128)}) custom-call(f32[256,512]{1,0:T(8,128)S(1)} %get-tuple-element.8.z0, f32[256,512]{1,0:T(8,128)S(1)} %get-tuple-element.9.y, f32[256,512]{1,0:T(8,128)S(1)} %get-tuple-element.10.r0, f32[256,512]{1,0:T(8,128)S(1)} %get-tuple-element.11.q, f32[256,512]{1,0:T(8,128)S(1)} %get-tuple-element.12.w, ...), custom_call_target="tpu_custom_call" | custom-call | tf_op jit(solution)/shard_map/combine/pallas_call | solution.py:799

commit v8 on v7

--- a/solution.py
+++ b/solution.py
@@ -633,7 +633,7 @@
     back16 = pick.T.astype(BF16)
 
     def stored(value):
-        return permuted(back16, value)
+        return sum(dot16(back16, part) for part in split(value, 2))
 
     sent_z0[...] = stored(field["z0"][...])
     sent_r0[...] = stored(r0_ref[...])

time: 28.4 us -> 28.4 us (level)
  no operation moved by 1% of the time
where the time goes in v8:
time: 28.4 us; the launch traced here: 28.3 us
  Pallas kernels  27.6 us (97%)
  between operations  0.64 us (2%)
    pallas_call x1, Pallas kernels, per_device(): pl.pallas_call(functools.partial(kernel, size), out_shape=(out,) * 5 + (s...  26.5 us
    pallas_call x1, Pallas kernels, per_device(): pl.pallas_call(combine, out_shape=(out, out), in_specs=[vmem] * 6, out_sp...  1.08 us

profile of v8, /device:TPU:1, one launch (start us, length us, event | category | flops | bytes accessed | tf_op | source)
XLA Modules:
  0.0 28.3 jit_solution(1301576919722429659)
XLA Ops:
  0.6 26.5 %solve.1 = (f32[256,512]{1,0:T(8,128)S(1)}, f32[256,512]{1,0:T(8,128)S(1)}, f32[256,512]{1,0:T(8,128)S(1)}, f32[256,512]{1,0:T(8,128)S(1)}, f32[256,512]{1,0:T(8,128)S(1)}, /*index=5*/f32[8,128]{1,0:T(8,128)S(1)}) custom-call(f32[256,512]{1,0:T(8,128)} %refs_0_.1, f32[1,256]{1,0:T(1,128)} %bitcast.1, s32[1,256]{1,0:T(1,128)} %refs_2_.1, ...), custom_call_target="tpu_custom_call" | custom-call | tf_op jit(solution)/shard_map/solve/pallas_call | solution.py:761
  27.2 1.1 %combine.1 = (f32[256,512]{1,0:T(8,128)}, f32[256,512]{1,0:T(8,128)}) custom-call(f32[256,512]{1,0:T(8,128)S(1)} %get-tuple-element.8.z0, f32[256,512]{1,0:T(8,128)S(1)} %get-tuple-element.9.y, f32[256,512]{1,0:T(8,128)S(1)} %get-tuple-element.10.r0, f32[256,512]{1,0:T(8,128)S(1)} %get-tuple-element.11.q, f32[256,512]{1,0:T(8,128)S(1)} %get-tuple-element.12.w, ...), custom_call_target="tpu_custom_call" | custom-call | tf_op jit(solution)/shard_map/combine/pallas_call | solution.py:799

commit v9 on v7

--- a/solution.py
+++ b/solution.py
@@ -427,7 +427,7 @@
     load_ref, r0_ref = field["load"], field["r0"]
 
     def permuted(matrix, value):
-        return sum(dot16(matrix, part) for part in split(value, 3))
+        return sum(dot16(matrix, part) for part in split(value, 2))
 
     for copy in forcing_loads[:2]:
         copy.wait()

time: 28.4 us -> 28.4 us (level)
  no operation moved by 1% of the time
where the time goes in v9:
time: 28.4 us; the launch traced here: 28.3 us
  Pallas kernels  27.6 us (97%)
  between operations  0.64 us (2%)
    pallas_call x1, Pallas kernels, per_device(): pl.pallas_call(functools.partial(kernel, size), out_shape=(out,) * 5 + (s...  26.5 us
    pallas_call x1, Pallas kernels, per_device(): pl.pallas_call(combine, out_shape=(out, out), in_specs=[vmem] * 6, out_sp...  1.08 us

profile of v9, /device:TPU:1, one launch (start us, length us, event | category | flops | bytes accessed | tf_op | source)
XLA Modules:
  0.0 28.3 jit_solution(18285324419418481457)
XLA Ops:
  0.6 26.5 %solve.1 = (f32[256,512]{1,0:T(8,128)S(1)}, f32[256,512]{1,0:T(8,128)S(1)}, f32[256,512]{1,0:T(8,128)S(1)}, f32[256,512]{1,0:T(8,128)S(1)}, f32[256,512]{1,0:T(8,128)S(1)}, /*index=5*/f32[8,128]{1,0:T(8,128)S(1)}) custom-call(f32[256,512]{1,0:T(8,128)} %refs_0_.1, f32[1,256]{1,0:T(1,128)} %bitcast.1, s32[1,256]{1,0:T(1,128)} %refs_2_.1, ...), custom_call_target="tpu_custom_call" | custom-call | tf_op jit(solution)/shard_map/solve/pallas_call | solution.py:761
  27.2 1.1 %combine.1 = (f32[256,512]{1,0:T(8,128)}, f32[256,512]{1,0:T(8,128)}) custom-call(f32[256,512]{1,0:T(8,128)S(1)} %get-tuple-element.8.z0, f32[256,512]{1,0:T(8,128)S(1)} %get-tuple-element.9.y, f32[256,512]{1,0:T(8,128)S(1)} %get-tuple-element.10.r0, f32[256,512]{1,0:T(8,128)S(1)} %get-tuple-element.11.q, f32[256,512]{1,0:T(8,128)S(1)} %get-tuple-element.12.w, ...), custom_call_target="tpu_custom_call" | custom-call | tf_op jit(solution)/shard_map/combine/pallas_call | solution.py:799
